TPU v7x, 128 devices: a whole 4x4x4 slice. The times are simulated.
128 devices in a mesh: seq: 64 (over x_lo, z, y, core), tp: 2 (over x_hi).
Axes of the slice: x: 4 (x_hi: 2, x_lo: 2; x = x_hi * 2 + x_lo), y: 4, z: 4, core: 2. Of those that a mesh axis runs over, the one named last changes fastest.
Arguments:
- tokens: bfloat16 [8192, 2048], P('seq'), may hold values from -6 to 6
- doc_lengths: int32 [2, 4], replicated, may hold values from 1 to 4000, as said below
- attn_gain: bfloat16 [2048], P('seq'), may hold values from 0.5 to 1.5
- q_weight: bfloat16 [2048, 2048], P('seq', 'tp'), may hold values from -0.125 to 0.125
- kv_weight: bfloat16 [2048, 256], P('seq'), may hold values from -0.125 to 0.125
- out_weight: bfloat16 [2048, 2048], P('tp', 'seq'), may hold values from -0.5 to 0.5
- ffn_gain: bfloat16 [2048], P('seq'), may hold values from 0.5 to 1.5
- gate_weight: bfloat16 [2048, 5632], P('seq', 'tp'), may hold values from -0.125 to 0.125
- up_weight: bfloat16 [2048, 5632], P('seq', 'tp'), may hold values from -0.125 to 0.125
- down_weight: bfloat16 [5632, 2048], P('tp', 'seq'), may hold values from -0.078125 to 0.078125
- second_queries: bfloat16 [8192, 2048], P('seq', 'tp'), may hold values from -8 to 8
- out_cotangent: bfloat16 [8192, 2048], P('seq'), may hold values from -6 to 6
- second_cotangent: bfloat16 [8192, 2048], P('seq', 'tp'), may hold values from -6 to 6
Outputs:
- result: float32 [8192, 2048], P('seq')
- second_out: float32 [8192, 2048], P('seq', 'tp')
- tokens_grad: float32 [8192, 2048], P('seq')
- attn_gain_grad: float32 [2048], P('seq')
- q_weight_grad: float32 [2048, 2048], P('seq', 'tp')
- kv_weight_grad: float32 [2048, 256], P('seq')
- out_weight_grad: float32 [2048, 2048], P('tp', 'seq')
- ffn_gain_grad: float32 [2048], P('seq')
- gate_weight_grad: float32 [2048, 5632], P('seq', 'tp')
- up_weight_grad: float32 [2048, 5632], P('seq', 'tp')
- down_weight_grad: float32 [5632, 2048], P('tp', 'seq')
- second_queries_grad: float32 [8192, 2048], P('seq', 'tp')
Inputs may be any that keep to these rules, and one draw needn't show every extreme that they name: `doc_lengths`: each row sums to 4096. In each row one document, at a place drawn from the seed, has exactly 4096 - 3 * (32) tokens; the other documents of the row together have (3) * (32) tokens, and one of them has exactly 1.
All inputs are finite; a program needn't handle non-finite values.
Results may differ from a plain program's by a relative error of at most 0.018.
Values may be sent and summed in bfloat16 or wider, within the bound.
No kernel may reach another device: no remote copies, remote signals or barrier semaphores. Data moves between devices by JAX's collectives and lax.ppermute only.
A program may use at most 256 MiB of HBM per device.

v0:
```python
import math

import jax
import jax.numpy as jnp
from jax import lax
from jax.sharding import PartitionSpec as P

SEQ_MIN = 4096


norm_eps = 1e-05
rope_base = 10000.0
masked_fill = -1e30


def shifted(block, axis, distance):
    devices = range(lax.axis_size(axis))
    route = [(i - distance, i) for i in devices if i - distance in devices]
    return lax.ppermute(block, axis, route)


def doc_layout(doc_lengths, first_index, count, seq_len):
    token_index = first_index + jnp.arange(count, dtype=jnp.int32)
    seq_index = token_index // seq_len
    place = token_index - seq_index * seq_len
    seq_count = doc_lengths.shape[0]
    doc_count = doc_lengths.shape[1]
    picked = (seq_index[:, None] == jnp.arange(seq_count, dtype=jnp.int32)[None, :]).astype(
        jnp.int32
    )
    row_lengths = jnp.sum(picked[:, :, None] * doc_lengths[None, :, :], axis=1)
    row_ends = jnp.cumsum(row_lengths, axis=1)
    passed = (place[:, None] >= row_ends).astype(jnp.int32)
    segment = seq_index * doc_count + jnp.sum(passed, axis=1)
    begins = jnp.sum(passed * row_lengths, axis=1)
    return (segment, place - begins)


def rotate(values_in, positions, sign):
    half_dim = values_in.shape[-1] // 2
    freq_index = jnp.arange(half_dim, dtype=jnp.float32)
    inverse_freq = jnp.exp(freq_index * (-2.0 * math.log(rope_base) / values_in.shape[-1]))
    angles = positions.astype(jnp.float32)[:, None] * inverse_freq[None, :]
    shape_out = (angles.shape[0],) + (1,) * (values_in.ndim - 2) + (half_dim,)
    cosine = jnp.cos(angles).reshape(shape_out)
    sine = (sign * jnp.sin(angles)).reshape(shape_out)
    first_half = values_in[..., :half_dim]
    second_half = values_in[..., half_dim:]
    return jnp.concatenate(
        [first_half * cosine - second_half * sine, second_half * cosine + first_half * sine],
        axis=-1,
    )


def to_rows(per_token):
    return jnp.transpose(per_token, (1, 0, 2)).reshape(-1, per_token.shape[2])


def from_rows(row_major, tok_rows):
    head_dim = row_major.shape[1]
    return jnp.transpose(row_major.reshape(-1, tok_rows, head_dim), (1, 0, 2)).reshape(tok_rows, -1)


def keep_state(previous):
    return previous


def on_device(
    tokens,
    doc_lengths,
    attn_gain,
    q_weight,
    kv_weight,
    out_weight,
    ffn_gain,
    gate_weight,
    up_weight,
    down_weight,
    second_queries,
    out_cotangent,
    second_cotangent,
):
    tok_rows = tokens.shape[0]
    head_dim = kv_weight.shape[1] // 2
    local_heads = q_weight.shape[1] // head_dim
    seq_len = min(SEQ_MIN, tok_rows * lax.axis_size("seq"))
    span = seq_len // tok_rows
    device = lax.axis_index("seq")
    first_row = device * tok_rows
    rank = device % span
    score_scale = head_dim ** (-0.5)
    segment, positions = doc_layout(doc_lengths, first_row, tok_rows, seq_len)
    gathered_rows = (
        lax.all_gather(q_weight, "seq", axis=0, tiled=True),
        lax.all_gather(kv_weight, "seq", axis=0, tiled=True),
        lax.all_gather(gate_weight, "seq", axis=0, tiled=True),
        lax.all_gather(up_weight, "seq", axis=0, tiled=True),
        lax.all_gather(attn_gain, "seq", axis=0, tiled=True),
        lax.all_gather(ffn_gain, "seq", axis=0, tiled=True),
    )
    gathered_cols = (
        lax.all_gather(out_weight, "seq", axis=1, tiled=True),
        lax.all_gather(down_weight, "seq", axis=1, tiled=True),
    )
    q_full, kv_full, gate_full, up_full, gain_attn, gain_ffn = gathered_rows
    out_full, down_full = gathered_cols
    gain_one = gain_attn.astype(jnp.float32)
    gain_two = gain_ffn.astype(jnp.float32)
    inputs = tokens.astype(jnp.float32)
    inv_attn = lax.rsqrt(jnp.mean(inputs * inputs, axis=-1, keepdims=True) + norm_eps)
    normed = (inputs * inv_attn * gain_one).astype(jnp.bfloat16)
    queries = jnp.dot(normed, q_full, preferred_element_type=jnp.float32)
    keyval = jnp.dot(normed, kv_full, preferred_element_type=jnp.float32)
    query_rot = rotate(queries.reshape(tok_rows, local_heads, head_dim), positions, 1.0).astype(
        jnp.bfloat16
    )
    key_rot = rotate(keyval[:, :head_dim], positions, 1.0).astype(jnp.bfloat16)
    value_rows = keyval[:, head_dim:].astype(jnp.bfloat16)
    query_rows = jnp.concatenate(
        [to_rows(query_rot), to_rows(second_queries.reshape(tok_rows, local_heads, head_dim))],
        axis=0,
    )
    row_count = query_rows.shape[0]
    row_index = jnp.tile(first_row + jnp.arange(tok_rows, dtype=jnp.int32), 2 * local_heads)
    row_segment = jnp.tile(segment, 2 * local_heads)

    def block_scores(block, distance):
        key_offset = first_row - distance * tok_rows
        key_segment, unused = doc_layout(doc_lengths, key_offset, tok_rows, seq_len)
        key_index = key_offset + jnp.arange(tok_rows, dtype=jnp.int32)
        allowed = (row_segment[:, None] == key_segment[None, :]) & (
            key_index[None, :] <= row_index[:, None]
        )
        scores = (
            jnp.einsum(
                "rd,kd->rk", query_rows, block[:, :head_dim], preferred_element_type=jnp.float32
            )
            * score_scale
        )
        return (allowed, scores)

    def gather_stats(running, block, distance):

        def gather_live_block(previous):
            row_top, row_mass = previous
            allowed, scores = block_scores(block, distance)
            masked = jnp.where(allowed, scores, masked_fill)
            new_top = jnp.maximum(row_top, jnp.max(masked, axis=-1))
            weights = jnp.where(allowed, jnp.exp(masked - new_top[:, None]), 0.0)
            return (new_top, row_mass * jnp.exp(row_top - new_top) + jnp.sum(weights, axis=-1))

        return lax.cond(distance <= rank, gather_live_block, keep_state, running)

    own_block = jnp.concatenate([key_rot, value_rows], axis=1)

    def cycle_step(carry, distance):
        running, block = carry
        running = gather_stats(running, block, distance)
        moved = shifted(block, "seq", 1)
        return ((running, moved), block)

    start_stats = (
        jnp.full((row_count,), masked_fill, jnp.float32),
        jnp.zeros((row_count,), jnp.float32),
    )
    (stats, last_block), kept_front = lax.scan(
        cycle_step, (start_stats, own_block), jnp.arange(span - 1, dtype=jnp.int32)
    )
    row_top, row_mass = gather_stats(stats, last_block, span - 1)
    kept = jnp.concatenate([kept_front, last_block[None]], axis=0)
    row_lse = row_top + jnp.log(row_mass)

    def block_probs(block, distance):
        allowed, scores = block_scores(block, distance)
        return jnp.where(
            allowed, jnp.exp(jnp.where(allowed, scores - row_lse[:, None], masked_fill)), 0.0
        )

    def out_step(acc, item):
        block, distance = item

        def out_live_block(previous):
            probs_low = block_probs(block, distance).astype(jnp.bfloat16)
            return previous + jnp.dot(
                probs_low, block[:, head_dim:], preferred_element_type=jnp.float32
            )

        return (lax.cond(distance <= rank, out_live_block, keep_state, acc), None)

    out_rows, unused = lax.scan(
        out_step,
        jnp.zeros((row_count, head_dim), jnp.float32),
        (kept, jnp.arange(span, dtype=jnp.int32)),
    )
    half_rows = row_count // 2
    attended = from_rows(out_rows[:half_rows], tok_rows).astype(jnp.bfloat16)
    second_out = from_rows(out_rows[half_rows:], tok_rows)
    branch = lax.psum(
        jnp.dot(attended, out_full, preferred_element_type=jnp.float32).astype(jnp.bfloat16), "tp"
    ).astype(jnp.float32)
    resid = inputs + branch
    inv_ffn = lax.rsqrt(jnp.mean(resid * resid, axis=-1, keepdims=True) + norm_eps)
    normed2 = (resid * inv_ffn * gain_two).astype(jnp.bfloat16)
    gate_pre = jnp.dot(normed2, gate_full, preferred_element_type=jnp.float32)
    up_pre = jnp.dot(normed2, up_full, preferred_element_type=jnp.float32)
    gate_sig = jax.nn.sigmoid(gate_pre)
    gate_act = gate_pre * gate_sig
    hidden = (gate_act * up_pre).astype(jnp.bfloat16)
    ffn_part = jnp.dot(hidden, down_full, preferred_element_type=jnp.float32)
    result = resid + lax.psum(ffn_part.astype(jnp.bfloat16), "tp").astype(jnp.float32)
    down_grad = jnp.einsum("ti,td->id", hidden, out_cotangent, preferred_element_type=jnp.float32)
    d_hidden = jnp.einsum("td,id->ti", out_cotangent, down_full, preferred_element_type=jnp.float32)
    d_gate = (d_hidden * up_pre * gate_sig * (1.0 + gate_pre * (1.0 - gate_sig))).astype(
        jnp.bfloat16
    )
    d_up = (d_hidden * gate_act).astype(jnp.bfloat16)
    gate_grad = jnp.einsum("td,ti->di", normed2, d_gate, preferred_element_type=jnp.float32)
    up_grad = jnp.einsum("td,ti->di", normed2, d_up, preferred_element_type=jnp.float32)
    d_norm_part = jnp.einsum(
        "ti,di->td", d_gate, gate_full, preferred_element_type=jnp.float32
    ) + jnp.einsum("ti,di->td", d_up, up_full, preferred_element_type=jnp.float32)
    d_normed2 = lax.psum(d_norm_part.astype(jnp.bfloat16), "tp").astype(jnp.float32)
    scaled_two = gain_two * d_normed2
    ffn_gain_part = jnp.sum(d_normed2 * resid * inv_ffn, axis=0)
    d_resid = (
        out_cotangent.astype(jnp.float32)
        + inv_ffn * scaled_two
        - resid * inv_ffn**3 * jnp.mean(scaled_two * resid, axis=-1, keepdims=True)
    )
    d_branch = d_resid.astype(jnp.bfloat16)
    out_grad = jnp.einsum("tj,td->jd", attended, d_branch, preferred_element_type=jnp.float32)
    d_attended = jnp.einsum(
        "td,jd->tj", d_branch, out_full, preferred_element_type=jnp.float32
    ).astype(jnp.bfloat16)
    d_out_rows = jnp.concatenate(
        [
            to_rows(d_attended.reshape(tok_rows, local_heads, head_dim)),
            to_rows(second_cotangent.reshape(tok_rows, local_heads, head_dim)),
        ],
        axis=0,
    )
    row_delta = jnp.sum(d_out_rows.astype(jnp.float32) * out_rows, axis=-1)

    def back_block(d_query_acc, distance):
        block = kept[distance]

        def back_live_block(previous):
            probs = block_probs(block, distance)
            d_probs = jnp.einsum(
                "rd,kd->rk", d_out_rows, block[:, head_dim:], preferred_element_type=jnp.float32
            )
            d_scores = (probs * (d_probs - row_delta[:, None])).astype(jnp.bfloat16)
            new_acc = (
                previous
                + jnp.dot(d_scores, block[:, :head_dim], preferred_element_type=jnp.float32)
                * score_scale
            )
            d_keys = (
                jnp.einsum("rk,rd->kd", d_scores, query_rows, preferred_element_type=jnp.float32)
                * score_scale
            )
            d_values = jnp.einsum(
                "rk,rd->kd",
                probs.astype(jnp.bfloat16),
                d_out_rows,
                preferred_element_type=jnp.float32,
            )
            return (new_acc, jnp.concatenate([d_keys, d_values], axis=1))

        def skip_block(previous):
            return (previous, jnp.zeros((tok_rows, 2 * head_dim), jnp.float32))

        return lax.cond(distance <= rank, back_live_block, skip_block, d_query_acc)

    first_query, first_term = back_block(jnp.zeros((row_count, head_dim), jnp.float32), span - 1)

    def return_step(carry, distance):
        d_query_acc, kv_acc = carry
        moved = shifted(kv_acc.astype(jnp.bfloat16), "seq", -1).astype(kv_acc.dtype)
        d_query_acc, kv_term = back_block(d_query_acc, distance)
        return ((d_query_acc, moved + kv_term), None)

    (d_query_rows, d_keyval_part), unused = lax.scan(
        return_step, (first_query, first_term), jnp.arange(span - 2, -1, -1, dtype=jnp.int32)
    )
    second_queries_grad = from_rows(d_query_rows[half_rows:], tok_rows)
    d_query_first = jnp.transpose(
        d_query_rows[:half_rows].reshape(local_heads, tok_rows, head_dim), (1, 0, 2)
    )
    d_queries = (
        rotate(d_query_first, positions, -1.0)
        .reshape(tok_rows, local_heads * head_dim)
        .astype(jnp.bfloat16)
    )
    d_norm_query = jnp.einsum("tj,dj->td", d_queries, q_full, preferred_element_type=jnp.float32)
    d_norm_sum, d_keyval_rows = (
        lax.psum(d_norm_query.astype(jnp.bfloat16), "tp").astype(jnp.float32),
        lax.psum(d_keyval_part.astype(jnp.bfloat16), "tp").astype(jnp.float32),
    )
    d_keyval = jnp.concatenate(
        [rotate(d_keyval_rows[:, :head_dim], positions, -1.0), d_keyval_rows[:, head_dim:]], axis=1
    ).astype(jnp.bfloat16)
    d_normed = d_norm_sum + jnp.einsum(
        "tk,dk->td", d_keyval, kv_full, preferred_element_type=jnp.float32
    )
    q_grad = jnp.einsum("td,tj->dj", normed, d_queries, preferred_element_type=jnp.float32)
    kv_grad = jnp.einsum("td,tk->dk", normed, d_keyval, preferred_element_type=jnp.float32)
    scaled_one = gain_one * d_normed
    attn_gain_part = jnp.sum(d_normed * inputs * inv_attn, axis=0)
    tokens_grad = (
        d_resid
        + inv_attn * scaled_one
        - inputs * inv_attn**3 * jnp.mean(scaled_one * inputs, axis=-1, keepdims=True)
    )
    row_grads = (
        lax.psum_scatter(q_grad, "seq", scatter_dimension=0, tiled=True),
        lax.psum_scatter(kv_grad, "seq", scatter_dimension=0, tiled=True),
        lax.psum_scatter(gate_grad, "seq", scatter_dimension=0, tiled=True),
        lax.psum_scatter(up_grad, "seq", scatter_dimension=0, tiled=True),
        lax.psum_scatter(attn_gain_part, "seq", scatter_dimension=0, tiled=True),
        lax.psum_scatter(ffn_gain_part, "seq", scatter_dimension=0, tiled=True),
    )
    col_grads = (
        lax.psum_scatter(out_grad, "seq", scatter_dimension=1, tiled=True),
        lax.psum_scatter(down_grad, "seq", scatter_dimension=1, tiled=True),
    )
    q_share, kv_share, gate_share, up_share, attn_gain_share, ffn_gain_share = row_grads
    out_share, down_share = col_grads
    return (
        result,
        second_out,
        tokens_grad,
        attn_gain_share,
        q_share,
        kv_share,
        out_share,
        ffn_gain_share,
        gate_share,
        up_share,
        down_share,
        second_queries_grad,
    )


def solution(mesh):
    in_specs = (
        P("seq", None),
        P(),
        P("seq"),
        P("seq", "tp"),
        P("seq", None),
        P("tp", "seq"),
        P("seq"),
        P("seq", "tp"),
        P("seq", "tp"),
        P("tp", "seq"),
        P("seq", "tp"),
        P("seq", None),
        P("seq", "tp"),
    )
    out_specs = (
        P("seq", None),
        P("seq", "tp"),
        P("seq", None),
        P("seq"),
        P("seq", "tp"),
        P("seq", None),
        P("tp", "seq"),
        P("seq"),
        P("seq", "tp"),
        P("seq", "tp"),
        P("tp", "seq"),
        P("seq", "tp"),
    )
    return jax.shard_map(
        on_device, mesh=mesh, in_specs=in_specs, out_specs=out_specs, check_vma=False
    )
```

profile of v0, /device:TPU:1, one launch (start us, length us, event | category | flops | bytes accessed | tf_op | source)
XLA Modules:
  0.0 3494.5 jit_solution(7415091268880229772)
XLA Ops:
  15.5 143.2 %all-reduce.5 = (bf16[2048]{0:T(1024)(128)(2,1)S(1)}, bf16[2048]{0:T(1024)(128)(2,1)S(1)}) all-reduce(bf16[2048]{0:T(1024)(128)(2,1)S(1)} %dynamic-update-slice, bf16[2048]{0:T(1024)(128)(2,1)S(1)} %dynamic-update-slice.1), channel_id=1, replica_groups=mesh['seq'=64,'tp'=2] {'seq'}, use_global_device_ids=true, to_apply=%add | all-reduce | flops 4096 | bytes 16384
  163.7 58.0 %all-gather.9.cloned.1.call-done = bf16[2048,1024]{1,0:T(8,128)(2,1)} async-done(((bf16[32,1024]{1,0:T(8,128)(2,1)}), bf16[2048,1024]{1,0:T(8,128)(2,1)}) %all-gather.9.cloned.1.call-update) | async-done | bytes 4194320 | tf_op jit(solution)/shard_map/all_gather | solution.py:94
  225.3 247.2 %while.47 = (s32[]{:T(128)}, f32[2048]{0:T(1024)S(1)}, f32[2048]{0:T(1024)S(1)}, bf16[128,256]{1,0:T(8,128)(2,1)S(1)}, bf16[31,128,256]{2,1,0:T(8,128)(2,1)S(1)}...) while((s32[]{:T(128)}, f32[2048]{0:T(1024)S(1)}, ...), condition=%wide.region_13.14_spmd.clone, body=%wide.region_5.13_spmd.clone.sunk | while | flops 70268416 | bytes 3351939 | solution.py:166
  249.4 5.8 collective-permute-start
  278.6 5.9 collective-permute-start
  336.7 5.8 collective-permute-start
  345.3 5.8 collective-permute-start
  353.8 5.7 collective-permute-start
  476.0 50.0 %while.48 = (s32[]{:T(128)}, f32[2048,128]{1,0:T(8,128)S(1)}, s32[32]{0:T(128)S(1)}, s32[]{:T(128)}, s32[]{:T(128)}, /*index=5*/s32[2,4]{1,0:T(2,128)}, bf16[32,...) while((s32[]{:T(128)}, f32[2048,128]{1,0:T(8,128)S(1)}, ...), condition=%wide.region_27.28_spmd.clone, body=%wide.region_21.27_spmd.clone.sunk | while | flops 136586752 | bytes 2875707 | solution.py:190
  534.5 254.5 %all-reduce.11.cloned.1.call-done = bf16[128,2048]{1,0:T(8,128)(2,1)} async-done(((bf16[128,2048]{1,0:T(8,128)(2,1)}), bf16[128,2048]{1,0:T(8,128)(2,1)}) %all-reduce.11.cloned.1.call-update) | async-done | bytes 524304 | tf_op jit(solution)/shard_map/psum | solution.py:198
  791.6 115.9 %all-gather.13.cloned.1.call-done = bf16[2048,2816]{1,0:T(8,128)(2,1)} async-done(((bf16[32,2816]{1,0:T(8,128)(2,1)}), bf16[2048,2816]{1,0:T(8,128)(2,1)}) %all-gather.13.cloned.1.call-update) | async-done | bytes 11534352 | tf_op jit(solution)/shard_map/all_gather | solution.py:96
  907.5 7.1 fusion.119
  914.6 110.5 %all-gather.15.cloned.1.call-done = bf16[2048,2816]{1,0:T(8,128)(2,1)} async-done(((bf16[32,2816]{1,0:T(8,128)(2,1)}), bf16[2048,2816]{1,0:T(8,128)(2,1)}) %all-gather.15.cloned.1.call-update) | async-done | bytes 11534352 | tf_op jit(solution)/shard_map/all_gather | solution.py:97
  1025.1 7.1 fusion.120
  1032.2 110.7 %all-gather.17.cloned.1.call-done = bf16[2816,2048]{0,1:T(8,128)(2,1)} async-done(((bf16[2816,32]{0,1:T(8,128)(2,1)}), bf16[2816,2048]{0,1:T(8,128)(2,1)}) %all-gather.17.cloned.1.call-update) | async-done | bytes 11534352 | tf_op jit(solution)/shard_map/all_gather | solution.py:103
  1142.9 8.2 multiply_convert_fusion
  1151.1 8.6 fusion.121
  1164.7 9.1 convolution_convert_fusion.1
  1173.8 25.9 all-reduce.13.cloned.1.call-done
  1206.6 249.6 %while.49 = (s32[]{:T(128)}, f32[2048,128]{1,0:T(8,128)S(1)}, bf16[128,256]{0,1:T(8,128)(2,1)}, s32[31]{0:T(128)}, s32[]{:T(128)}, /*index=5*/s32[]{:T(128)}, s3...) while((s32[]{:T(128)}, f32[2048,128]{1,0:T(8,128)S(1)}, ...), condition=%wide.region_45.46_spmd.clone, body=%wide.region_39.45_spmd.clone.sunk | while | flops 339109376 | bytes 10125741 | solution.py:283
  1435.8 7.6 conditional.15
  1447.9 7.6 conditional.15
  1464.7 177.0 %all-reduce.15.cloned.1.call-done = (bf16[128,2048]{1,0:T(8,128)(2,1)}, bf16[128,2048]{1,0:T(8,128)(2,1)}, bf16[128,256]{1,0:T(8,128)(2,1)}) async-done(((bf16[128,2048]{1,0:T(8,128)(2,1)}, bf16[128,2048]{1,0:T(8,128)(2,1)}, bf16[128,256]{1,0:T(8,128)(2,1)}), (bf16[128,2048]{1,0:T(8,128)(2,1)}, bf16[128,2048]{1,0:T(8,128)(2,1)}, bf16[128,256]{1,0:T(8,128)(2,1)})) %all-reduce.15.cloned.1.call-update) | async-done | bytes 1114128 | tf_op jit(solution)/shard_map/psum | solution.py:210
  1656.7 10.5 fusion.122
  1667.3 10.4 fusion.123
  1678.8 9.3 fusion.124
  1694.1 273.7 %all-reduce.4 = (f32[2048]{0:T(1024)S(1)}, f32[2048]{0:T(1024)S(1)}) all-reduce(f32[2048]{0:T(1024)S(1)} %get-tuple-element.586, f32[2048]{0:T(1024)S(1)} %copy-done.22), channel_id=2, replica_groups=mesh['seq'=64,'tp'=2] {'seq'}, use_global_device_ids=true, to_apply=%region_50.51.clone | all-reduce | flops 4096 | bytes 32768
  1972.8 251.3 %reduce-scatter.7.cloned.1.call-done = f32[32,1024]{1,0:T(8,128)} async-done(((f32[2048,1024]{1,0:T(8,128)}), f32[32,1024]{1,0:T(8,128)}) %reduce-scatter.7.cloned.1.call-update) | async-done | bytes 131088 | tf_op jit(solution)/shard_map/reduce_scatter | solution.py:316
  2224.1 297.4 %reduce-scatter.11.cloned.1.call-done = f32[1024,32]{0,1:T(8,128)} async-done(((f32[1024,2048]{0,1:T(8,128)}), f32[1024,32]{0,1:T(8,128)}) %reduce-scatter.11.cloned.1.call-update) | async-done | bytes 131088 | tf_op jit(solution)/shard_map/reduce_scatter | solution.py:324
  2521.4 322.3 %reduce-scatter.13.cloned.1.call-done = f32[32,2816]{1,0:T(8,128)} async-done(((f32[2048,2816]{1,0:T(8,128)}), f32[32,2816]{1,0:T(8,128)}) %reduce-scatter.13.cloned.1.call-update) | async-done | bytes 360464 | tf_op jit(solution)/shard_map/reduce_scatter | solution.py:318
  2843.7 321.9 %reduce-scatter.15.cloned.1.call-done = f32[32,2816]{1,0:T(8,128)} async-done(((f32[2048,2816]{1,0:T(8,128)}), f32[32,2816]{1,0:T(8,128)}) %reduce-scatter.15.cloned.1.call-update) | async-done | bytes 360464 | tf_op jit(solution)/shard_map/reduce_scatter | solution.py:319
  3165.6 321.9 %reduce-scatter.17.cloned.1.call-done = f32[2816,32]{0,1:T(8,128)} async-done(((f32[2816,2048]{0,1:T(8,128)}), f32[2816,32]{0,1:T(8,128)}) %reduce-scatter.17.cloned.1.call-update) | async-done | bytes 360464 | tf_op jit(solution)/shard_map/reduce_scatter | solution.py:325
  (694 shorter events, 539.9 us)
Async XLA Ops:
  7.2 153.6 %all-gather.7.cloned.1.call-start = ((), (), s32[]{:S(2)}) async-start(), calls=%async_computation.6 | async-start | bytes 1064960 | tf_op jit(solution)/shard_map/all_gather | solution.py:95
  7.9 213.7 %all-gather.9.cloned.1.call-start = ((), (), s32[]{:S(2)}) async-start(), calls=%async_computation.7 | async-start | bytes 4259840 | tf_op jit(solution)/shard_map/all_gather | solution.py:94
  8.7 517.5 %all-gather.11.cloned.1.call-start = ((), (), s32[]{:S(2)}) async-start(), calls=%async_computation.8 | async-start | bytes 4259840 | tf_op jit(solution)/shard_map/all_gather | solution.py:102
  9.4 779.6 %all-reduce.11.cloned.1.call-start = ((), (), s32[]{:S(2)}) async-start(), calls=%async_computation.9 | async-start | bytes 1048576 | tf_op jit(solution)/shard_map/psum | solution.py:198
  226.0 8.5 collective-permute-start
  235.1 7.9 collective-permute-start
  249.4 8.0 collective-permute-start
  278.6 8.0 collective-permute-start
  345.3 7.9 collective-permute-start
  531.0 376.5 %all-gather.13.cloned.1.call-start = ((), (), s32[]{:S(2)}) async-start(), calls=%async_computation.10 | async-start | bytes 11714560 | tf_op jit(solution)/shard_map/all_gather | solution.py:96
  531.6 493.5 %all-gather.15.cloned.1.call-start = ((), (), s32[]{:S(2)}) async-start(), calls=%async_computation.11 | async-start | bytes 11714560 | tf_op jit(solution)/shard_map/all_gather | solution.py:97
  532.2 610.7 %all-gather.17.cloned.1.call-start = ((), (), s32[]{:S(2)}) async-start(), calls=%async_computation.12 | async-start | bytes 11714560 | tf_op jit(solution)/shard_map/all_gather | solution.py:103
  532.9 666.8 %all-reduce.13.cloned.1.call-start = ((), (), s32[]{:S(2)}) async-start(), calls=%async_computation.13 | async-start | bytes 1048576 | tf_op jit(solution)/shard_map/psum | solution.py:222
  1164.4 477.3 %all-reduce.15.cloned.1.call-start = ((), (), s32[]{:S(2)}) async-start(), calls=%async_computation.20 | async-start | bytes 2228224 | tf_op jit(solution)/shard_map/psum | solution.py:210
  1278.3 7.9 collective-permute-start.1
  1286.9 7.9 collective-permute-start.1
  1295.4 7.9 collective-permute-start.1
  1303.9 7.9 collective-permute-start.1
  1312.5 7.9 collective-permute-start.1
  1321.0 7.9 collective-permute-start.1
  1329.5 7.9 collective-permute-start.1
  1338.1 7.9 collective-permute-start.1
  1363.7 7.9 collective-permute-start.1
  1397.9 7.9 collective-permute-start.1
  1432.0 11.4 collective-permute-start.1
  1444.1 11.4 collective-permute-start.1
  1464.6 508.1 %reduce-scatter.9.cloned.1.call-start = ((), (), s32[]{:S(2)}) async-start(), calls=%async_computation.15 | async-start | bytes 2129920 | tf_op jit(solution)/shard_map/reduce_scatter | solution.py:317
  1645.6 578.4 %reduce-scatter.7.cloned.1.call-start = ((), (), s32[]{:S(2)}) async-start(), calls=%async_computation.14 | async-start | bytes 8519680 | tf_op jit(solution)/shard_map/reduce_scatter | solution.py:316
  1650.4 871.0 %reduce-scatter.11.cloned.1.call-start = ((), (), s32[]{:S(2)}) async-start(), calls=%async_computation.16 | async-start | bytes 8519680 | tf_op jit(solution)/shard_map/reduce_scatter | solution.py:324
  1656.6 1187.1 %reduce-scatter.13.cloned.1.call-start = ((), (), s32[]{:S(2)}) async-start(), calls=%async_computation.17 | async-start | bytes 23429120 | tf_op jit(solution)/shard_map/reduce_scatter | solution.py:318
  1667.2 1498.3 %reduce-scatter.15.cloned.1.call-start = ((), (), s32[]{:S(2)}) async-start(), calls=%async_computation.18 | async-start | bytes 23429120 | tf_op jit(solution)/shard_map/reduce_scatter | solution.py:319
  1677.7 1809.7 %reduce-scatter.17.cloned.1.call-start = ((), (), s32[]{:S(2)}) async-start(), calls=%async_computation.19 | async-start | bytes 23429120 | tf_op jit(solution)/shard_map/reduce_scatter | solution.py:325
  (83 other events, 6315.2 us)
Sparse Core Ops, SparseCore 0:
  9.8 105.1 all-gather.6
  116.7 104.9 all-gather.8
  223.4 106.1 all-gather.10
  531.1 257.8 all-reduce.10
  790.7 116.7 all-gather.12
  909.2 115.8 all-gather.14
  1027.0 115.8 all-gather.16
  1164.5 35.1 all-reduce.12
  1464.7 176.9 all-reduce.14
  1645.8 280.5 reduce-scatter.8
  1929.3 294.6 reduce-scatter.6
  2226.9 294.4 reduce-scatter.10
  2524.4 319.2 reduce-scatter.12
  2846.5 319.0 reduce-scatter.14
  3168.4 319.0 reduce-scatter.16
where the time goes:
time: 3520 us; the launch traced here: 3490 us
  waiting for transfers between devices  2470 us (70%)
  blocking collectives  417 us (12%)
  starting transfers between devices  215 us (6%)
  local copies, waits for them, and re-layouts  147 us (4%)
  matrix products  115 us (3%)
  loops' own time  73.8 us (2%)
  other arithmetic  44.9 us (1%)
    unnamed x2, blocking collectives  417 us
    reduce_scatter x1, waiting for transfers between devices, on_device(): lax.psum_scatter(gate_grad, 'seq', scatter_dimension=0, tiled=True)  322 us
    reduce_scatter x1, waiting for transfers between devices, on_device(): lax.psum_scatter(up_grad, 'seq', scatter_dimension=0, tiled=True)  322 us
    reduce_scatter x1, waiting for transfers between devices, on_device(): lax.psum_scatter(down_grad, 'seq', scatter_dimension=1, tiled=True)  322 us
    reduce_scatter x1, waiting for transfers between devices, on_device(): lax.psum_scatter(out_grad, 'seq', scatter_dimension=1, tiled=True)  297 us
    psum x1, waiting for transfers between devices, on_device(): lax.psum(jnp.dot(attended, out_full, preferred_element_type=jnp.float32)....  255 us
    reduce_scatter x1, waiting for transfers between devices, on_device(): lax.psum_scatter(q_grad, 'seq', scatter_dimension=0, tiled=True)  251 us
    ppermute x62, starting transfers between devices, shifted(): return lax.ppermute(block, axis, route)  213 us
  transfers between devices with their start and end apart: 77, of which 41 were waited for; matrix products, arithmetic and copies ran while one was open for 7% of the time, Pallas kernels for 0%

commit v1 on v0

v1 whole, which is shorter than its diff:
```python
import functools
import math

import jax
import jax.numpy as jnp
from jax import lax
from jax.experimental import pallas as pl
from jax.experimental.pallas import tpu as pltpu
from jax.sharding import Mesh, PartitionSpec as P

norm_eps = 1e-05
rope_base = 10000.0
masked_fill = -1e30
KEY_BLOCK = 1024
BF = jnp.bfloat16
F32 = jnp.float32
MB = 1024 * 1024


def fetch(block, axis, offset):
    n = lax.axis_size(axis)
    return lax.ppermute(block, axis, [((i + offset) % n, i) for i in range(n)])


def hand(block, axis, offset):
    return fetch(block, axis, -offset)


def in_order(first, mine, other, axis):
    return jnp.where(
        first,
        jnp.concatenate([mine, other], axis=axis),
        jnp.concatenate([other, mine], axis=axis),
    )


X, Z, Y = 0, 1, 2


def gather_first(piece):
    both = jnp.stack([piece, fetch(piece, "x", 1)], axis=1)
    width = piece.shape[-1]
    halves = []
    for h, axis in ((0, "z"), (1, "y")):
        mine = both[h].reshape(-1, width)
        halves.append(jnp.concatenate([mine] + [fetch(mine, axis, d) for d in (1, 2, 3)], axis=0))
    return halves


def gather_second(halves):
    by_z, by_y = halves
    zero = [by_z] + [fetch(by_z, "y", d) for d in (1, 2, 3)]
    return zero + [by_y] + [fetch(by_y, "z", d) for d in (1, 2, 3)]


def group_place(pos_ref, group):
    h, y, z, x = group % 2, group // 2 % 4, group // 8 % 4, group // 32
    dx = lax.rem(x - pos_ref[X] + 2, 2)
    dz = lax.rem(z - pos_ref[Z] + 4, 4)
    dy = lax.rem(y - pos_ref[Y] + 4, 4)
    one, two = (dy, dz) if h == 0 else (dz, dy)
    return h * 4 + one, two * 2 + dx


def turned(pos, act):
    toks, feats = act.shape

    def kernel(pos_ref, act_ref, out_ref):
        for block in range(feats // 128):
            part = act_ref[:, block * 128 : (block + 1) * 128].T
            for k in range(4):
                chunk, at = group_place(pos_ref, block * 4 + k)
                out_ref[chunk, at] = part[k * 32 : (k + 1) * 32]

    return pl.pallas_call(
        kernel,
        in_specs=[
            pl.BlockSpec(memory_space=pltpu.SMEM),
            pl.BlockSpec(memory_space=pltpu.VMEM),
        ],
        out_specs=pl.BlockSpec(memory_space=pltpu.VMEM),
        out_shape=jax.ShapeDtypeStruct((8, 8, 32, toks), act.dtype),
        compiler_params=pltpu.CompilerParams(vmem_limit_bytes=16 * MB),
        cost_estimate=pl.CostEstimate(
            flops=0, bytes_accessed=4 * toks * feats, transcendentals=0
        ),
        name="turned",
    )(pos, act).reshape(8, 256, toks)


def turn_back(pos_ref, wide_ref, out_ref):
    for block in range(16):
        groups = [wide_ref[group_place(pos_ref, block * 4 + k)] for k in range(4)]
        rows = jnp.concatenate(groups, axis=0)
        out_ref[:, block * 128 : (block + 1) * 128] = rows.T.astype(out_ref.dtype)


SMEM_SPEC = pl.BlockSpec(memory_space=pltpu.SMEM)
VMEM_SPEC = pl.BlockSpec(memory_space=pltpu.VMEM)


def project(act, chunks, columns, dtypes, flips):
    toks = act.shape[-1]
    width = sum(columns)

    def kernel(act_ref, *refs):
        weights, outs = refs[:8], refs[8:]
        total = jnp.zeros((toks, width), F32)
        for k in range(8):
            total = total + jnp.dot(
                act_ref[k].T, weights[k][:, :width], preferred_element_type=F32
            )
        begin = 0
        for out, w, flip in zip(outs, columns, flips):
            part = total[:, begin : begin + w]
            out[...] = (part.T if flip else part).astype(out.dtype)
            begin += w

    shapes = [(w, toks) if flip else (toks, w) for w, flip in zip(columns, flips)]
    return pl.pallas_call(
        kernel,
        in_specs=[VMEM_SPEC] * 9,
        out_specs=[VMEM_SPEC] * len(columns),
        out_shape=[jax.ShapeDtypeStruct(s, t) for s, t in zip(shapes, dtypes)],
        compiler_params=pltpu.CompilerParams(vmem_limit_bytes=32 * MB),
        cost_estimate=pl.CostEstimate(
            flops=2 * toks * 2048 * width, bytes_accessed=2 * 2048 * (width + toks), transcendentals=0
        ),
        name="project",
    )(act, *chunks)


def unproject(pos, chunks, sides):
    toks = sides[0][0].shape[0 if sides[0][1] else 1]
    count = len(sides)

    def kernel(pos_ref, *refs):
        rights, weights, out_ref, wide = refs[:count], refs[count : count + 8], refs[-2], refs[-1]
        for k in range(8):
            total = None
            begin = 0
            for right, (side, flipped) in zip(rights, sides):
                w = side.shape[1] if flipped else side.shape[0]
                dims = (((1,), (1 if flipped else 0,)), ((), ()))
                part = lax.dot_general(
                    weights[k][:, begin : begin + w], right[...], dims, preferred_element_type=F32
                )
                total = part if total is None else total + part
                begin += w
            wide[k] = total.reshape(8, 32, toks)
        turn_back(pos_ref, wide, out_ref)

    width = chunks[0].shape[1]
    return pl.pallas_call(
        kernel,
        in_specs=[SMEM_SPEC] + [VMEM_SPEC] * (count + 8),
        out_specs=VMEM_SPEC,
        out_shape=jax.ShapeDtypeStruct((toks, 2048), BF),
        scratch_shapes=[pltpu.VMEM((8, 8, 32, toks), F32)],
        compiler_params=pltpu.CompilerParams(vmem_limit_bytes=32 * MB),
        cost_estimate=pl.CostEstimate(
            flops=2 * toks * 2048 * width, bytes_accessed=2 * 2048 * (width + toks), transcendentals=0
        ),
        name="unproject",
    )(pos, *[s for s, f in sides], *chunks)


TILE = 128


def feed_forward(pos, normed2, cot, chunks):
    toks = normed2.shape[-1]
    tiles = chunks[0].shape[1] // (3 * TILE)
    wide_pair = 2 * TILE

    def kernel(pos_ref, normed_ref, cot_ref, *refs):
        weights, grads = refs[:8], refs[8:16]
        ffn_ref, d_norm_ref = refs[16:18]
        normed_rows, cot_rows, pair_weights, down_weights, pair_side, hidden_side, wide = refs[18:]
        j = pl.program_id(0)

        @pl.when(j == 0)
        def _():
            for k in range(8):
                normed_rows[k] = normed_ref[k].T
                cot_rows[k] = cot_ref[k].T

        pre = jnp.zeros((toks, wide_pair), F32)
        d_hidden = jnp.zeros((toks, TILE), F32)
        for k in range(8):
            pre = pre + jnp.dot(
                normed_rows[k], weights[k][:, :wide_pair], preferred_element_type=F32
            )
            d_hidden = d_hidden + jnp.dot(
                cot_rows[k], weights[k][:, wide_pair:], preferred_element_type=F32
            )
        gate, up = pre[:, :TILE], pre[:, TILE:]
        gate_sig = jax.nn.sigmoid(gate)
        gate_act = gate * gate_sig
        hidden = (gate_act * up).astype(BF)
        d_gate = (d_hidden * up * gate_sig * (1.0 + gate * (1.0 - gate_sig))).astype(BF)
        d_up = (d_hidden * gate_act).astype(BF)
        d_pair = jnp.concatenate([d_gate, d_up], axis=1)
        for k in range(8):
            grads[k][:, :wide_pair] = jnp.dot(
                normed_ref[k], d_pair, preferred_element_type=F32
            ).astype(BF)
            grads[k][:, wide_pair:] = jnp.dot(
                cot_ref[k], hidden, preferred_element_type=F32
            ).astype(BF)
        pair_at = pl.ds(pl.multiple_of(j * wide_pair, wide_pair), wide_pair)
        tile_at = pl.ds(pl.multiple_of(j * TILE, TILE), TILE)
        pair_side[:, pair_at] = d_pair
        hidden_side[:, tile_at] = hidden
        for k in range(8):
            pair_weights[k, :, pair_at] = weights[k][:, :wide_pair]
            down_weights[k, :, tile_at] = weights[k][:, wide_pair:]

        @pl.when(j == tiles - 1)
        def _():
            dims = (((1,), (1,)), ((), ()))
            for out_ref, left, right in (
                (d_norm_ref, pair_weights, pair_side),
                (ffn_ref, down_weights, hidden_side),
            ):
                for k in range(8):
                    wide[k] = lax.dot_general(
                        left[k], right[...], dims, preferred_element_type=F32
                    ).reshape(8, 32, toks)
                turn_back(pos_ref, wide, out_ref)

    whole = pl.BlockSpec((8, 256, toks), lambda j: (0, 0, 0))
    tile = pl.BlockSpec((256, 3 * TILE), lambda j: (0, j))
    rows = pl.BlockSpec((toks, 2048), lambda j: (0, 0))
    width = chunks[0].shape[1]
    outs = pl.pallas_call(
        kernel,
        grid=(tiles,),
        in_specs=[SMEM_SPEC, whole, whole] + [tile] * 8,
        out_specs=[tile] * 8 + [rows] * 2,
        out_shape=[jax.ShapeDtypeStruct((256, width), BF)] * 8
        + [jax.ShapeDtypeStruct((toks, 2048), BF)] * 2,
        scratch_shapes=[
            pltpu.VMEM((8, toks, 256), BF),
            pltpu.VMEM((8, toks, 256), BF),
            pltpu.VMEM((8, 256, tiles * wide_pair), BF),
            pltpu.VMEM((8, 256, tiles * TILE), BF),
            pltpu.VMEM((toks, tiles * wide_pair), BF),
            pltpu.VMEM((toks, tiles * TILE), BF),
            pltpu.VMEM((8, 8, 32, toks), F32),
        ],
        compiler_params=pltpu.CompilerParams(vmem_limit_bytes=56 * MB),
        cost_estimate=pl.CostEstimate(
            flops=6 * toks * 2048 * width, bytes_accessed=4 * 2048 * width, transcendentals=toks * width
        ),
        name="feed_forward",
    )(pos, normed2, cot, *chunks)
    return outs[:8], outs[8], outs[9]


def tiled(gate, up, down):
    lead = gate.shape[:-1]
    parts = [w.reshape(lead + (-1, 1, TILE)) for w in (gate, up, down)]
    return jnp.concatenate(parts, axis=-2).reshape(lead + (-1,))


def untiled(columns):
    lead = columns.shape[:-1]
    parts = columns.reshape(lead + (-1, 3, TILE))
    return [parts[..., i, :].reshape(lead + (-1,)) for i in range(3)]


SEND_ORDER = (1, 5, 3, 7, 2, 6, 0, 4)


def weight_chunks(terms, extra=None):
    lefts = []
    for left, right, flipped in terms:
        if not any(left is l for l in lefts):
            lefts.append(left)
    which = [next(i for i, l in enumerate(lefts) if l is left) for left, r, f in terms]
    widths = [r.shape[0] if f else r.shape[1] for l, r, f in terms]
    total = sum(widths) + (extra.shape[-1] if extra is not None else 0)
    operands = lefts + [r for l, r, f in terms] + ([extra] if extra is not None else [])
    count = len(operands)

    def kernel(*refs):
        ins, outs, slots, sem = refs[:count], refs[count : count + 8], refs[-2], refs[-1]
        copies = []
        for step, chunk in enumerate(SEND_ORDER):
            slot = step % 2
            if step >= 2:
                copies[step - 2].wait()
            begin = 0
            for i, (left, right, flipped) in enumerate(terms):
                dims = (((1,), (1 if flipped else 0,)), ((), ()))
                product = lax.dot_general(
                    ins[which[i]][chunk],
                    ins[len(lefts) + i][...],
                    dims,
                    preferred_element_type=F32,
                )
                slots[slot, :, begin : begin + widths[i]] = product.astype(BF)
                begin += widths[i]
            if extra is not None:
                slots[slot, :, begin:total] = ins[-1][chunk]
            copy = pltpu.make_async_copy(slots.at[slot], outs[chunk], sem.at[slot])
            copy.start()
            copies.append(copy)
        copies[-2].wait()
        copies[-1].wait()

    vmem = pl.BlockSpec(memory_space=pltpu.VMEM)
    flops = 2 * 2048 * 256 * total
    return pl.pallas_call(
        kernel,
        in_specs=[vmem] * count,
        out_specs=[pl.BlockSpec(memory_space=pl.ANY)] * 8,
        out_shape=[jax.ShapeDtypeStruct((256, total), BF)] * 8,
        scratch_shapes=[pltpu.VMEM((2, 256, total), BF), pltpu.SemaphoreType.DMA((2,))],
        compiler_params=pltpu.CompilerParams(vmem_limit_bytes=40 * MB),
        cost_estimate=pl.CostEstimate(
            flops=flops, bytes_accessed=2 * 2048 * total, transcendentals=0
        ),
        name="weight_chunks",
    )(*operands)


def summed(parts):
    total = parts[0].astype(F32)
    for part in parts[1:]:
        total = total + part.astype(F32)
    return total


def scatter_first(chunks):
    got = []
    for h, axis in ((0, "y"), (1, "z")):
        own = chunks[4 * h]
        got.append([own] + [hand(chunks[4 * h + d], axis, d) for d in (1, 2, 3)])
    return got


def scatter_second(got):
    width = got[0][0].shape[-1]
    shares = []
    for h, axis in ((0, "z"), (1, "y")):
        blocks = []
        for d in range(4):
            blocks.append(summed([g[d * 64 : (d + 1) * 64] for g in got[h]]).astype(BF))
        shares.append(
            [blocks[0]] + [hand(blocks[d], axis, d) for d in (1, 2, 3)]
        )
    keep = jnp.stack([summed([b[:32] for b in share]) for share in shares])
    give = jnp.stack([summed([b[32:] for b in share]).astype(BF) for share in shares])
    return keep + fetch(give, "x", 1).astype(F32)


def halves_of_rows(first, both):
    mine = jnp.where(first, both[0], both[1])
    give = jnp.where(first, both[1], both[0])
    return mine, fetch(give, "c", 1)


def allowed_keys(begin, count, info):
    shape = (count, info.shape[1])
    key_place = begin + lax.broadcasted_iota(jnp.int32, shape, 0)
    return (key_place <= info[0:1, :]) & (key_place >= info[1:2, :])


def attend_kernel(bounds, info_ref, qt_ref, k_ref, vt_ref, ot_ref, lse_ref, *, first_set, scale):
    units, head_dim, rows = qt_ref.shape
    at = jnp.where(pl.program_id(0) * units >= first_set, 2, 0)
    info = info_ref[0]

    def step(j, carry):
        begin = pl.multiple_of(j * KEY_BLOCK, KEY_BLOCK)
        keys = k_ref[pl.ds(begin, KEY_BLOCK), :]
        values = vt_ref[:, pl.ds(begin, KEY_BLOCK)]
        allowed = allowed_keys(begin, KEY_BLOCK, info)
        out = []
        for u in range(units):
            top, mass, acc = carry[u]
            scores = jnp.dot(keys, qt_ref[u], preferred_element_type=F32)
            scores = jnp.where(allowed, scores, masked_fill)
            new_top = jnp.maximum(top, jnp.max(scores, axis=0, keepdims=True))
            weights = jnp.exp2((scores - new_top) * scale)
            shrink = jnp.exp2((top - new_top) * scale)
            mass = mass * shrink + jnp.sum(weights, axis=0, keepdims=True)
            acc = acc * shrink + jnp.dot(
                values, weights.astype(BF), preferred_element_type=F32
            )
            out.append((new_top, mass, acc))
        return tuple(out)

    start = (
        jnp.full((1, rows), masked_fill, F32),
        jnp.zeros((1, rows), F32),
        jnp.zeros((head_dim, rows), F32),
    )
    done = lax.fori_loop(bounds[at], bounds[at + 1], step, (start,) * units)
    for u in range(units):
        top, mass, acc = done[u]
        ot_ref[u] = acc / mass
        lse_ref[u] = top * scale + jnp.log2(mass)


def attend(bounds, info, qt, keys, values_t, scale):
    units = 2
    blocks, head_dim, rows = qt.shape
    count = keys.shape[0]
    first_set = blocks // 2
    block = pl.BlockSpec((units, head_dim, rows), lambda i, b: (i, 0, 0))
    return pl.pallas_call(
        functools.partial(attend_kernel, first_set=first_set, scale=scale),
        grid_spec=pltpu.PrefetchScalarGridSpec(
            num_scalar_prefetch=1,
            grid=(blocks // units,),
            in_specs=[
                pl.BlockSpec((1, 2, rows), lambda i, b: (i * units // first_set, 0, 0)),
                block,
                pl.BlockSpec((count, head_dim), lambda i, b: (0, 0)),
                pl.BlockSpec((head_dim, count), lambda i, b: (0, 0)),
            ],
            out_specs=[block, pl.BlockSpec((units, 1, rows), lambda i, b: (i, 0, 0))],
        ),
        out_shape=[
            jax.ShapeDtypeStruct((blocks, head_dim, rows), F32),
            jax.ShapeDtypeStruct((blocks, 1, rows), F32),
        ],
        compiler_params=pltpu.CompilerParams(vmem_limit_bytes=48 * MB),
        cost_estimate=pl.CostEstimate(
            flops=8 * blocks * rows * count * head_dim,
            bytes_accessed=blocks * rows * head_dim * 6 + count * head_dim * 4,
            transcendentals=blocks * rows * count,
        ),
        name="attend",
    )(bounds, info, qt, keys, values_t)


def attend_back_kernel(
    bounds, info_ref, qt_ref, dot_ref, ot_ref, lse_ref, k_ref, kt_ref, v_ref, dqt_ref, dk_ref, dv_ref,
    *, first_set, scale,
):
    units, head_dim, rows = qt_ref.shape

    @pl.when(pl.program_id(0) == 0)
    def _():
        dk_ref[...] = jnp.zeros_like(dk_ref)
        dv_ref[...] = jnp.zeros_like(dv_ref)

    at = jnp.where(pl.program_id(0) * units >= first_set, 2, 0)
    info = info_ref[0]
    queries = [qt_ref[u].T for u in range(units)]
    d_outs = [dot_ref[u].T for u in range(units)]
    deltas = [
        jnp.sum(dot_ref[u].astype(F32) * ot_ref[u], axis=0, keepdims=True) for u in range(units)
    ]

    def step(j, carry):
        begin = pl.multiple_of(j * KEY_BLOCK, KEY_BLOCK)
        part = pl.ds(begin, KEY_BLOCK)
        allowed = allowed_keys(begin, KEY_BLOCK, info)
        out = []
        d_keys = d_values = None
        for u in range(units):
            scores = jnp.dot(k_ref[part, :], qt_ref[u], preferred_element_type=F32)
            d_probs = jnp.dot(v_ref[part, :], dot_ref[u], preferred_element_type=F32)
            probs = jnp.where(allowed, jnp.exp2(scores * scale - lse_ref[u]), 0.0)
            d_scores = (probs * (d_probs - deltas[u])).astype(BF)
            for_keys = jnp.dot(d_scores, queries[u], preferred_element_type=F32)
            for_values = jnp.dot(probs.astype(BF), d_outs[u], preferred_element_type=F32)
            d_keys = for_keys if u == 0 else d_keys + for_keys
            d_values = for_values if u == 0 else d_values + for_values
            out.append(
                carry[u] + jnp.dot(kt_ref[:, part], d_scores, preferred_element_type=F32)
            )
        dk_ref[part, :] += d_keys
        dv_ref[part, :] += d_values
        return tuple(out)

    start = jnp.zeros((head_dim, rows), F32)
    done = lax.fori_loop(bounds[at], bounds[at + 1], step, (start,) * units)
    for u in range(units):
        dqt_ref[u] = done[u]


def attend_back(bounds, info, qt, d_out_t, out_t, lse, keys, keys_t, values, scale):
    units = 2
    blocks, head_dim, rows = qt.shape
    count = keys.shape[0]
    first_set = blocks // 2
    block = pl.BlockSpec((units, head_dim, rows), lambda i, b: (i, 0, 0))
    whole = pl.BlockSpec((count, head_dim), lambda i, b: (0, 0))
    return pl.pallas_call(
        functools.partial(attend_back_kernel, first_set=first_set, scale=scale),
        grid_spec=pltpu.PrefetchScalarGridSpec(
            num_scalar_prefetch=1,
            grid=(blocks // units,),
            in_specs=[
                pl.BlockSpec((1, 2, rows), lambda i, b: (i * units // first_set, 0, 0)),
                block,
                block,
                block,
                pl.BlockSpec((units, 1, rows), lambda i, b: (i, 0, 0)),
                whole,
                pl.BlockSpec((head_dim, count), lambda i, b: (0, 0)),
                whole,
            ],
            out_specs=[block, whole, whole],
        ),
        out_shape=[jax.ShapeDtypeStruct((blocks, head_dim, rows), F32)]
        + [jax.ShapeDtypeStruct((count, head_dim), F32)] * 2,
        compiler_params=pltpu.CompilerParams(vmem_limit_bytes=56 * MB),
        cost_estimate=pl.CostEstimate(
            flops=10 * blocks * rows * count * head_dim,
            bytes_accessed=blocks * rows * head_dim * 12 + count * head_dim * 14,
            transcendentals=blocks * rows * count,
        ),
        name="attend_back",
    )(bounds, info, qt, d_out_t, out_t, lse, keys, keys_t, values)


def doc_starts(lengths, places):
    ends = jnp.cumsum(lengths)
    passed = (places[:, None] >= ends[None, :]).astype(jnp.int32)
    return jnp.sum(passed * lengths[None, :], axis=1)


def rotate_rows(values, cosine, sine):
    half = values.shape[-1] // 2
    one, two = values[..., :half], values[..., half:]
    return jnp.concatenate([one * cosine - two * sine, two * cosine + one * sine], axis=-1)


def rotate_columns(values, cosine, sine):
    half = values.shape[1] // 2
    one, two = values[:, :half], values[:, half:]
    return jnp.concatenate([one * cosine - two * sine, two * cosine + one * sine], axis=1)


def head_blocks(array):
    toks = array.shape[0]
    turned_rows = array.T.reshape(-1, 2, 128, toks)
    return jnp.transpose(turned_rows, (0, 2, 1, 3)).reshape(-1, 128, 2 * toks)


def head_blocks_back(blocks):
    count, head_dim, wide = blocks.shape
    rows = jnp.transpose(blocks.reshape(count, head_dim, 2, wide // 2), (0, 2, 1, 3))
    return rows.reshape(-1, wide // 2).T


def on_device(
    tokens, doc_lengths, attn_gain, q_weight, kv_weight, out_weight, ffn_gain,
    gate_weight, up_weight, down_weight, second_queries, out_cotangent, second_cotangent,
):
    x, z, y, c = (lax.axis_index(a) for a in ("x", "z", "y", "c"))
    first = c == 0
    pos = jnp.stack([x, z, y, c]).astype(jnp.int32)
    toks, width = tokens.shape
    head_dim = kv_weight.shape[1] // 2
    score_scale = head_dim ** (-0.5)
    scale = score_scale * math.log2(math.e)
    rows = q_weight.shape[0]

    def split(weights):
        mine = jnp.concatenate([jnp.where(first, a, b) for a, b in weights], axis=1)
        give = jnp.concatenate([jnp.where(first, b, a) for a, b in weights], axis=1)
        other = fetch(give, "c", 1)
        return jnp.where(first, jnp.stack([mine, other]), jnp.stack([other, mine]))

    def halved(w):
        return w[:, : w.shape[1] // 2], w[:, w.shape[1] // 2 :]

    n_q, n_kv = q_weight.shape[1] // 2, head_dim
    n_out, n_ffn = out_weight.shape[0] // 2, down_weight.shape[0] // 2
    gains = jnp.stack([attn_gain, ffn_gain], axis=1)
    gains = jnp.pad(gains, ((0, 0), (0, 126)))
    one = split([halved(q_weight), halved(kv_weight), (gains, gains)])
    two = split([halved(out_weight.T)])
    ffn_weights = [halved(w) for w in (gate_weight, up_weight, down_weight.T)]
    three = split([tuple(tiled(*[w[i] for w in ffn_weights]) for i in range(2))])

    one_halves = gather_first(one)
    attn_chunks = gather_second(one_halves)
    two_halves = gather_first(two)
    three_halves = gather_first(three)
    out_chunks = gather_second(two_halves)
    ffn_chunks = gather_second(three_halves)

    gain_cols = jnp.stack([w[:, n_q + n_kv : n_q + n_kv + 2] for w in attn_chunks])
    gain_cols = gain_cols.reshape(2, 4, 4, 2, 32, 2)
    here = lambda a, i, n, axis: jnp.take(a, (jnp.arange(n) - i) % n, axis=axis)
    gain_cols = jnp.stack(
        [
            jnp.transpose(here(here(here(gain_cols[0], y, 4, 0), z, 4, 1), x, 2, 2), (2, 1, 0, 3, 4)),
            jnp.transpose(here(here(here(gain_cols[1], z, 4, 0), y, 4, 1), x, 2, 2), (2, 0, 1, 3, 4)),
        ],
        axis=3,
    )
    gain_rows = gain_cols.reshape(-1, 2).T.astype(F32)
    gain_one, gain_two = gain_rows[0:1], gain_rows[1:2]

    def pair_up(own):
        return in_order(first, own, fetch(own, "c", 1), 0)

    def reduce_rows(partial):
        low = partial
        mine = jnp.where(first, low[:toks], low[toks:])
        give = jnp.where(first, low[toks:], low[:toks])
        core_sum = mine.astype(F32) + fetch(give, "c", 1).astype(F32)
        send = core_sum.astype(BF)
        return send.astype(F32) + fetch(send, "t", 1).astype(F32), core_sum

    chip = z * 4 + y
    pair_places = chip * (2 * toks) + jnp.arange(2 * toks, dtype=jnp.int32)
    lengths = jnp.where(x == 0, doc_lengths[0], doc_lengths[1])
    pair_starts = doc_starts(lengths, pair_places)
    positions = (pair_places - pair_starts).astype(F32)
    own_places = jnp.where(first, pair_places[:toks], pair_places[toks:])
    own_starts = jnp.where(first, pair_starts[:toks], pair_starts[toks:])
    info = jnp.stack(
        [
            jnp.stack([pair_places, pair_starts]),
            jnp.stack([jnp.tile(own_places, 2), jnp.tile(own_starts, 2)]),
        ]
    )
    bounds = jnp.stack(
        [
            pair_starts[0] // KEY_BLOCK,
            pair_places[-1] // KEY_BLOCK + 1,
            own_starts[0] // KEY_BLOCK,
            own_places[-1] // KEY_BLOCK + 1,
        ]
    ).astype(jnp.int32)
    inverse_freq = jnp.exp(
        jnp.arange(head_dim // 2, dtype=F32) * (-2.0 * math.log(rope_base) / head_dim)
    )
    angles_t = inverse_freq[:, None] * positions[None, :]
    cos_t, sin_t = jnp.cos(angles_t), jnp.sin(angles_t)
    cos_r, sin_r = cos_t.T, sin_t.T

    inputs = tokens.astype(F32)
    inv_attn = lax.rsqrt(jnp.mean(inputs * inputs, axis=-1, keepdims=True) + norm_eps)
    normed = pair_up((inputs * inv_attn * gain_one).astype(BF))
    normed_t = turned(pos, normed)
    queries_t, keyval = project(normed_t, attn_chunks, (n_q, n_kv), (F32, F32), (True, False))
    query_rot = rotate_columns(queries_t.reshape(-1, head_dim, 2 * toks), cos_t, sin_t).astype(BF)
    kv_own = jnp.where(first, rotate_rows(keyval, cos_r, sin_r), keyval).astype(BF)
    roll = lambda blocks, i: jnp.take(jnp.stack(blocks), (jnp.arange(4) - i) % 4, axis=0)
    kv_z = roll([kv_own] + [fetch(kv_own, "z", d) for d in (1, 2, 3)], z)
    kv_all = roll([kv_z] + [fetch(kv_z, "y", d) for d in (1, 2, 3)], y)
    kv_all = jnp.swapaxes(kv_all, 0, 1).reshape(-1, head_dim)
    kv_other = fetch(kv_all, "c", 1)
    keys = jnp.where(first, kv_all, kv_other)
    values = jnp.where(first, kv_other, kv_all)
    keys_t, values_t = keys.T, values.T
    query_t = jnp.concatenate([query_rot, head_blocks(second_queries)], axis=0)
    out_t, lse = attend(bounds, info, query_t, keys, values_t, scale)
    n_first = query_rot.shape[0]
    second_out = head_blocks_back(out_t[n_first:])
    attended_t = out_t[:n_first].reshape(-1, 2 * toks).astype(BF)

    branch, unused = reduce_rows(unproject(pos, out_chunks, [(attended_t, False)]))
    resid = inputs + branch
    inv_ffn = lax.rsqrt(jnp.mean(resid * resid, axis=-1, keepdims=True) + norm_eps)
    normed2 = pair_up((resid * inv_ffn * gain_two).astype(BF))
    cot = pair_up(out_cotangent)
    ffn_grads, ffn_part, d_norm2_part = feed_forward(
        pos, turned(pos, normed2), turned(pos, cot), ffn_chunks
    )
    ffn_got = scatter_first(ffn_grads)
    d_normed2, unused = reduce_rows(d_norm2_part)
    ffn_sum, unused = reduce_rows(ffn_part)
    result = resid + ffn_sum

    scaled_two = gain_two * d_normed2
    ffn_gain_part = jnp.sum(d_normed2 * resid * inv_ffn, axis=0)
    d_resid = (
        out_cotangent.astype(F32)
        + inv_ffn * scaled_two
        - resid * inv_ffn**3 * jnp.mean(scaled_two * resid, axis=-1, keepdims=True)
    )
    d_branch = pair_up(d_resid.astype(BF))

    d_branch_t = turned(pos, d_branch)
    (d_attended_t,) = project(d_branch_t, out_chunks, (n_out,), (BF,), (True,))
    d_out_t = jnp.concatenate(
        [d_attended_t.reshape(-1, head_dim, 2 * toks), head_blocks(second_cotangent)], axis=0
    )
    out_got = scatter_first(weight_chunks([(d_branch_t, attended_t, True)]))
    d_query_t, d_keys, d_values = attend_back(
        bounds, info, query_t, d_out_t, out_t, lse, keys, keys_t, values, scale
    )
    d_query_t = d_query_t * score_scale
    second_queries_grad = head_blocks_back(d_query_t[n_first:])
    d_queries_t = rotate_columns(d_query_t[:n_first], cos_t, -sin_t).reshape(-1, 2 * toks).astype(BF)

    d_keys = d_keys * score_scale
    kv_mine = jnp.where(first, d_keys, d_values)
    kv_give = jnp.where(first, d_values, d_keys).astype(BF)
    kv_chip = (kv_mine + fetch(kv_give, "c", 1).astype(F32)).reshape(4, 4, 2 * toks, head_dim)

    def pick(array, index):
        return lax.dynamic_index_in_dim(array, lax.rem(index, 4), 0, keepdims=False)

    kv_sum = summed(
        [pick(kv_chip, z)] + [hand(pick(kv_chip, z + d).astype(BF), "z", d) for d in (1, 2, 3)]
    )
    kv_sum = summed(
        [pick(kv_sum, y)] + [hand(pick(kv_sum, y + d).astype(BF), "y", d) for d in (1, 2, 3)]
    )
    d_keyval = jnp.where(first, rotate_rows(kv_sum, cos_r, -sin_r), kv_sum).astype(BF)
    d_norm_part = unproject(pos, attn_chunks, [(d_queries_t, False), (d_keyval, True)])
    d_normed, d_norm_core = reduce_rows(d_norm_part)
    attn_gain_part = jnp.sum(d_norm_core * inputs * inv_attn, axis=0)

    gain_parts = jnp.stack([attn_gain_part, 0.5 * ffn_gain_part]).reshape(2, 2, 4, 4, 2, 32)
    take = lambda a, i, n, axis: jnp.take(a, (i + jnp.arange(n)) % n, axis=axis)
    gain_parts = take(take(take(gain_parts, x, 2, 1), z, 4, 2), y, 4, 3)
    gain_chunks = jnp.stack(
        [
            jnp.transpose(gain_parts[:, :, :, :, 0], (3, 2, 1, 4, 0)),
            jnp.transpose(gain_parts[:, :, :, :, 1], (2, 3, 1, 4, 0)),
        ]
    ).reshape(8, 256, 2)
    gain_chunks = jnp.pad(gain_chunks, ((0, 0), (0, 0), (0, 126))).astype(BF)
    attn_got = scatter_first(
        weight_chunks(
            [(normed_t, d_queries_t, True), (normed_t, d_keyval, False)],
            gain_chunks,
        )
    )
    scaled_one = gain_one * d_normed
    tokens_grad = (
        d_resid
        + inv_attn * scaled_one
        - inputs * inv_attn**3 * jnp.mean(scaled_one * inputs, axis=-1, keepdims=True)
    )

    def whole_rows(got, widths):
        mine, other = halves_of_rows(first, scatter_second(got))
        shares = []
        begin = 0
        for w in widths:
            part = slice(begin, begin + w)
            shares.append((mine[:, part], other[:, part]))
            begin += w
        return shares

    (ffn_s,) = whole_rows(ffn_got, (3 * n_ffn,))
    gate_s, up_s, down_s = zip(*[untiled(side) for side in ffn_s])
    (out_s,) = whole_rows(out_got, (n_out,))
    q_s, kv_s, gain_s = whole_rows(attn_got, (n_q, n_kv, 128))
    joined = lambda s: in_order(first, s[0], s[1], 1)
    kv_gain = jnp.concatenate([joined(kv_s), gain_s[0] + gain_s[1]], axis=1)
    kv_gain = kv_gain + fetch(kv_gain, "t", 1)
    return (
        result,
        second_out,
        tokens_grad,
        kv_gain[:, 2 * n_kv],
        joined(q_s),
        kv_gain[:, : 2 * n_kv],
        joined(out_s).T,
        kv_gain[:, 2 * n_kv + 1],
        joined(gate_s),
        joined(up_s),
        joined(down_s).T,
        second_queries_grad,
    )


def solution(mesh):
    fine = Mesh(mesh.devices.reshape(2, 4, 4, 2, 2), ("x", "z", "y", "c", "t"))
    seq = ("x", "z", "y", "c")
    rows, both, turned_both = P(seq, None), P(seq, "t"), P("t", seq)
    in_specs = (
        rows, P(), P(seq), both, rows, turned_both, P(seq), both, both, turned_both, both, rows, both,
    )
    out_specs = (
        rows, both, rows, P(seq), both, rows, turned_both, P(seq), both, both, turned_both, both,
    )
    return jax.shard_map(
        on_device, mesh=fine, in_specs=in_specs, out_specs=out_specs, check_vma=False
    )
```

time: 3520 us -> 842 us (0.24)
  waiting for transfers between devices: 2470 us -> 358 us
  blocking collectives: 417 us -> 0 us
  matrix products: 115 us -> 0 us
  loops' own time: 73.8 us -> 0 us
  local copies, waits for them, and re-layouts: 147 us -> 73.5 us
  Pallas kernels: 0 us -> 67.1 us
  starting transfers between devices: 215 us -> 253 us
    reduce_scatter x6 -> x0, waiting for transfers between devices: 1510 us -> none  [the longest x1 322 us: on_device(): lax.psum_scatter(gate_grad, 'seq', scatter_dimension=0, tiled=True)]
    psum x3 -> x0, waiting for transfers between devices: 458 us -> none  [the longest x1 255 us: on_device(): lax.psum(jnp.dot(attended, out_full, preferred_element_type=jnp.float32)....]
    unnamed x2 -> x0, blocking collectives: 417 us -> none
    all_gather x6 -> x0, waiting for transfers between devices: 395 us -> none  [the longest x1 116 us: on_device(): lax.all_gather(gate_weight, 'seq', axis=0, tiled=True)]
    ppermute x62 -> x111, waiting for transfers between devices: 94.2 us -> 358 us  [fetch(): return lax.ppermute(block, axis, [((i + offset) % n, i) for i in range(n)])]
    dot_general x32 -> x0, matrix products: 115 us -> none  [the longest x1 10.5 us: on_device(): jnp.einsum('td,ti->di', normed2, d_gate, preferred_element_type=jnp.float32)]
    dynamic_slice x94 -> x0, local copies, waits for them, and re-layouts: 75.4 us -> none  [the longest x62 56.7 us: on_device(): lax.scan(cycle_step, (start_stats, own_block), jnp.arange(span - 1, dtype...]
    another operation x99 -> x0, loops' own time: 73.8 us -> none  [the longest x1 21.7 us: on_device(): lax.scan(out_step, jnp.zeros((row_count, head_dim), jnp.float32), (kept,...]
  transfers between devices with their start and end apart: 77 -> 111, of which waited for: 41 -> 45; matrix products, arithmetic and copies ran while one was open for 7% -> 14% of each run, Pallas kernels for 0% -> 4%
where the time goes in v1:
time: 842 us; the launch traced here: 831 us
  waiting for transfers between devices  358 us (43%)
  starting transfers between devices  253 us (30%)
  local copies, waits for them, and re-layouts  73.5 us (9%)
  other arithmetic  68.3 us (8%)
  Pallas kernels  67.1 us (8%)
  between operations  10.8 us (1%)
    ppermute x111, waiting for transfers between devices, fetch(): return lax.ppermute(block, axis, [((i + offset) % n, i) for i in range(n)])  358 us
    ppermute x111, starting transfers between devices, fetch(): return lax.ppermute(block, axis, [((i + offset) % n, i) for i in range(n)])  253 us
    pallas_call x1, Pallas kernels, feed_forward(): pl.pallas_call(kernel, grid=(tiles,), in_specs=[SMEM_SPEC, whole, whole]...  29.1 us
  transfers between devices with their start and end apart: 111, of which 45 were waited for; matrix products, arithmetic and copies ran while one was open for 14% of the time, Pallas kernels for 4%

profile of v1, /device:TPU:1, one launch (start us, length us, event | category | flops | bytes accessed | tf_op | source)
XLA Modules:
  0.0 831.4 jit_solution(10385462891742128352)
XLA Ops:
  68.1 12.3 %collective-permute-start.40 = (bf16[32,4224]{1,0:T(8,128)(2,1)}, bf16[32,4224]{1,0:T(8,128)(2,1)}, u32[]{:S(2)}, u32[]{:S(2)}) collective-permute-start(bf16[32,4224]{1,0:T(8,128)(2,1)} %select_n.648), channel_id=1, source_target_pairs={{2,0},{0,2},{3,1},{1,3},{6,4},{4,6},{7,5},{5,7},{10,8},{8,10},{11,... | collective-permute-start | bytes 811016 | tf_op jit(solution)/shard_map/ppermute | solution.py:22
  129.7 6.4 collective-permute-done.20
  158.3 7.1 attend.1
  168.4 5.6 collective-permute-start.36
  174.0 8.6 %collective-permute-done.50 = bf16[64,4224]{1,0:T(8,128)(2,1)S(1)} collective-permute-done((bf16[64,4224]{1,0:T(8,128)(2,1)}, bf16[64,4224]{1,0:T(8,128)(2,1)S(1)}, u32[]{:S(2)}, u32[]{:S(2)}) %collective-permute-start.50) | collective-permute-done | bytes 540704 | tf_op jit(solution)/shard_map/ppermute | solution.py:22
  182.8 11.9 %collective-permute-start.51 = (bf16[256,4224]{1,0:T(8,128)(2,1)S(1)}, bf16[256,4224]{1,0:T(8,128)(2,1)S(1)}, u32[]{:S(2)}, u32[]{:S(2)}) collective-permute-start(bf16[256,4224]{1,0:T(8,128)(2,1)S(1)} %pad_maximum_fusion.1.refs_4_), channel_id=1, source_target_pairs={{16,0},{32,16},{48,32},{0,48},{17,1},{33,17},{49,33},{1,49},{18,2}... | collective-permute-start | bytes 6488072 | tf_op jit(solution)/shard_map/ppermute | solution.py:22
  199.7 10.1 %collective-permute-done.37 = bf16[128,2048]{1,0:T(8,128)(2,1)S(1)} collective-permute-done((bf16[128,2048]{1,0:T(8,128)(2,1)S(1)}, bf16[128,2048]{1,0:T(8,128)(2,1)S(1)}, u32[]{:S(2)}, u32[]{:S(2)}) %collective-permute-start.37) | collective-permute-done | bytes 524320 | tf_op jit(solution)/shard_map/ppermute | solution.py:22
  211.3 53.1 %collective-permute-done.42 = bf16[64,4224]{1,0:T(8,128)(2,1)S(1)} collective-permute-done((bf16[64,4224]{1,0:T(8,128)(2,1)S(1)}, bf16[64,4224]{1,0:T(8,128)(2,1)S(1)}, u32[]{:S(2)}, u32[]{:S(2)}) %collective-permute-start.42) | collective-permute-done | bytes 540704 | tf_op jit(solution)/shard_map/ppermute | solution.py:22
  278.5 35.1 %collective-permute-done.52.refs_6_ = bf16[256,4224]{1,0:T(8,128)(2,1)S(1)} collective-permute-done((bf16[256,4224]{1,0:T(8,128)(2,1)S(1)}, bf16[256,4224]{1,0:T(8,128)(2,1)S(1)}, u32[]{:S(2)}, u32[]{:S(2)}) %collective-permute-start.52) | collective-permute-done | bytes 2162720 | tf_op jit(solution)/shard_map/ppermute | solution.py:22
  313.6 47.5 %collective-permute-done.53.refs_7_ = bf16[256,4224]{1,0:T(8,128)(2,1)S(1)} collective-permute-done((bf16[256,4224]{1,0:T(8,128)(2,1)S(1)}, bf16[256,4224]{1,0:T(8,128)(2,1)S(1)}, u32[]{:S(2)}, u32[]{:S(2)}) %collective-permute-start.53) | collective-permute-done | bytes 2162720 | tf_op jit(solution)/shard_map/ppermute | solution.py:22
  361.1 8.0 collective-permute-done.47.refs_3_
  370.5 29.1 %feed_forward.1 = (bf16[256,4224]{1,0:T(8,128)(2,1)}, bf16[256,4224]{1,0:T(8,128)(2,1)}, bf16[256,4224]{1,0:T(8,128)(2,1)}, bf16[256,4224]{1,0:T(8,128)(2,1)}, b...) custom-call(s32[4]{0:T(128)} %copy-done.32, ...), custom_call_target="tpu_custom_call" | custom-call | flops 13287555072 | bytes 34603008 | tf_op jit(solution)/shard_map/feed_forward/pallas_call | solution.py:236
  415.5 9.6 %collective-permute-done.57 = bf16[128,2048]{1,0:T(8,128)(2,1)S(1)} collective-permute-done((bf16[128,2048]{1,0:T(8,128)(2,1)S(1)}, bf16[128,2048]{1,0:T(8,128)(2,1)S(1)}, u32[]{:S(2)}, u32[]{:S(2)}) %collective-permute-start.57) | collective-permute-done | bytes 524320 | tf_op jit(solution)/shard_map/ppermute | solution.py:22
  425.5 10.8 %collective-permute-done.55 = bf16[128,2048]{1,0:T(8,128)(2,1)S(1)} collective-permute-done((bf16[128,2048]{1,0:T(8,128)(2,1)S(1)}, bf16[128,2048]{1,0:T(8,128)(2,1)S(1)}, u32[]{:S(2)}, u32[]{:S(2)}) %collective-permute-start.55) | collective-permute-done | bytes 524320 | tf_op jit(solution)/shard_map/ppermute | solution.py:22
  465.5 36.9 %collective-permute-done.83 = bf16[256,512]{1,0:T(8,128)(2,1)} collective-permute-done((bf16[256,512]{1,0:T(8,128)(2,1)}, bf16[256,512]{1,0:T(8,128)(2,1)}, u32[]{:S(2)}, u32[]{:S(2)}) %collective-permute-start.83) | collective-permute-done | bytes 262176 | tf_op jit(solution)/shard_map/ppermute | solution.py:22
  507.3 12.2 %attend_back.1 = (f32[8,128,256]{2,1,0:T(8,128)}, f32[4096,128]{1,0:T(8,128)}, f32[4096,128]{1,0:T(8,128)}) custom-call(s32[4]{0:T(128)} %copy-done.35, s32[2,2,256]{2,1,0:T(2,128)} %copy-done.34, bf16[8,128,256]{2,1,0:T(8,128)(2,1)} %pad_maximum_fusion.5.qt_ref, bf16[8,128,256]{2,1,0:T(8,128)(2,1)} %pad_maximum_fusion.6.dot_ref, f32[8,128,256]{2,1,0:T(8,128)} %copy-done.23, ...), custom_call_target="tpu_custom_call" | custom-call | flops 10737418240 | bytes 10485760 | tf_op jit(solution)/shard_map/attend_back/pallas_call | solution.py:495
  521.6 7.9 collective-permute-start.86
  529.4 13.1 %collective-permute-start.87 = (bf16[64,512]{1,0:T(8,128)(2,1)S(1)}, bf16[64,512]{1,0:T(8,128)(2,1)S(1)}, u32[]{:S(2)}, u32[]{:S(2)}) collective-permute-start(bf16[64,512]{1,0:T(8,128)(2,1)S(1)} %get-tuple-element.130), channel_id=1, source_target_pairs={{32,0},{48,16},{0,32},{16,48},{33,1},{49,17},{1,33},{17,49},{34,2}... | collective-permute-start | bytes 196616 | tf_op jit(solution)/shard_map/ppermute | solution.py:22
  548.3 24.1 %collective-permute-done.92 = bf16[64,512]{1,0:T(8,128)(2,1)S(1)} collective-permute-done((bf16[64,512]{1,0:T(8,128)(2,1)S(1)}, bf16[64,512]{1,0:T(8,128)(2,1)S(1)}, u32[]{:S(2)}, u32[]{:S(2)}) %collective-permute-start.92) | collective-permute-done | bytes 65568 | tf_op jit(solution)/shard_map/ppermute | solution.py:22
  572.4 7.8 collective-permute-start.103
  584.5 13.1 %collective-permute-start.104 = (bf16[256,4224]{1,0:T(8,128)(2,1)}, bf16[256,4224]{1,0:T(8,128)(2,1)}, u32[]{:S(2)}, u32[]{:S(2)}) collective-permute-start(bf16[256,4224]{1,0:T(8,128)(2,1)} %get-tuple-element.79), channel_id=1, source_target_pairs={{32,0},{48,16},{0,32},{16,48},{33,1},{49,17},{1,33},{17,49},{34,2}... | collective-permute-start | bytes 6488072 | tf_op jit(solution)/shard_map/ppermute | solution.py:22
  607.5 13.4 %collective-permute-done.99 = bf16[256,4224]{1,0:T(8,128)(2,1)} collective-permute-done((bf16[256,4224]{1,0:T(8,128)(2,1)}, bf16[256,4224]{1,0:T(8,128)(2,1)}, u32[]{:S(2)}, u32[]{:S(2)}) %collective-permute-start.99) | collective-permute-done | bytes 2162720 | tf_op jit(solution)/shard_map/ppermute | solution.py:22
  622.2 4.6 add_convert_fusion.7
  626.8 11.8 %collective-permute-done.103 = bf16[256,4224]{1,0:T(8,128)(2,1)} collective-permute-done((bf16[256,4224]{1,0:T(8,128)(2,1)}, bf16[256,4224]{1,0:T(8,128)(2,1)}, u32[]{:S(2)}, u32[]{:S(2)}) %collective-permute-start.103) | collective-permute-done | bytes 2162720 | tf_op jit(solution)/shard_map/ppermute | solution.py:22
  638.6 39.6 %collective-permute-start.100 = (bf16[64,4224]{1,0:T(8,128)(2,1)S(1)}, bf16[64,4224]{1,0:T(8,128)(2,1)S(1)}, u32[]{:S(2)}, u32[]{:S(2)}) collective-permute-start(bf16[64,4224]{1,0:T(8,128)(2,1)S(1)} %get-tuple-element.100), channel_id=1, source_target_pairs={{48,0},{0,16},{16,32},{32,48},{49,1},{1,17},{17,33},{33,49},{50,2}... | collective-permute-start | bytes 1622024 | tf_op jit(solution)/shard_map/ppermute | solution.py:22
  678.2 7.7 collective-permute-done.104
  685.9 6.3 collective-permute-done.105
  702.5 6.5 collective-permute-done.101
  718.2 6.8 collective-permute-done.107
  739.7 7.0 collective-permute-start.66
  791.9 4.6 collective-permute-done.69
  814.4 7.9 collective-permute-start.81
  (658 shorter events, 334.0 us)
Async XLA Ops:
  34.2 33.8 %collective-permute-start.12 = (bf16[256,768]{1,0:T(8,128)(2,1)S(1)}, bf16[256,768]{1,0:T(8,128)(2,1)S(1)}, u32[]{:S(2)}, u32[]{:S(2)}) collective-permute-start(bf16[256,768]{1,0:T(8,128)(2,1)S(1)} %pad_maximum_fusion.8.refs_4_.refs_6_), channel_id=1, source_target_pairs={{32,0},{48,16},{0,32},{16,48},{33,1},{49,17},{1,33},{17,49},{34,2}... | collective-permute-start | bytes 1179656 | tf_op jit(solution)/shard_map/ppermute | solution.py:22
  41.8 38.7 %collective-permute-start.13 = (bf16[256,768]{1,0:T(8,128)(2,1)S(1)}, bf16[256,768]{1,0:T(8,128)(2,1)S(1)}, u32[]{:S(2)}, u32[]{:S(2)}) collective-permute-start(bf16[256,768]{1,0:T(8,128)(2,1)S(1)} %pad_maximum_fusion.8.refs_4_.refs_6_), channel_id=1, source_target_pairs={{48,0},{0,16},{16,32},{32,48},{49,1},{1,17},{17,33},{33,49},{50,2}... | collective-permute-start | bytes 1179656 | tf_op jit(solution)/shard_map/ppermute | solution.py:22
  41.8 38.9 %collective-permute-start.5 = (bf16[256,768]{1,0:T(8,128)(2,1)S(1)}, bf16[256,768]{1,0:T(8,128)(2,1)S(1)}, u32[]{:S(2)}, u32[]{:S(2)}) collective-permute-start(bf16[256,768]{1,0:T(8,128)(2,1)S(1)} %pad_maximum_fusion.7.refs_0_.refs_2_), channel_id=1, source_target_pairs={{4,0},{8,4},{12,8},{0,12},{5,1},{9,5},{13,9},{1,13},{6,2},{10,6},{... | collective-permute-start | bytes 1179656 | tf_op jit(solution)/shard_map/ppermute | solution.py:22
  43.5 37.4 %collective-permute-start.6 = (bf16[256,768]{1,0:T(8,128)(2,1)S(1)}, bf16[256,768]{1,0:T(8,128)(2,1)S(1)}, u32[]{:S(2)}, u32[]{:S(2)}) collective-permute-start(bf16[256,768]{1,0:T(8,128)(2,1)S(1)} %pad_maximum_fusion.7.refs_0_.refs_2_), channel_id=1, source_target_pairs={{8,0},{12,4},{0,8},{4,12},{9,1},{13,5},{1,9},{5,13},{10,2},{14,6},... | collective-permute-start | bytes 1179656 | tf_op jit(solution)/shard_map/ppermute | solution.py:22
  43.6 37.5 %collective-permute-start.7 = (bf16[256,768]{1,0:T(8,128)(2,1)S(1)}, bf16[256,768]{1,0:T(8,128)(2,1)S(1)}, u32[]{:S(2)}, u32[]{:S(2)}) collective-permute-start(bf16[256,768]{1,0:T(8,128)(2,1)S(1)} %pad_maximum_fusion.7.refs_0_.refs_2_), channel_id=1, source_target_pairs={{12,0},{0,4},{4,8},{8,12},{13,1},{1,5},{5,9},{9,13},{14,2},{2,6},{... | collective-permute-start | bytes 1179656 | tf_op jit(solution)/shard_map/ppermute | solution.py:22
  68.1 52.2 %collective-permute-start.40 = (bf16[32,4224]{1,0:T(8,128)(2,1)}, bf16[32,4224]{1,0:T(8,128)(2,1)}, u32[]{:S(2)}, u32[]{:S(2)}) collective-permute-start(bf16[32,4224]{1,0:T(8,128)(2,1)} %select_n.648), channel_id=1, source_target_pairs={{2,0},{0,2},{3,1},{1,3},{6,4},{4,6},{7,5},{5,7},{10,8},{8,10},{11,... | collective-permute-start | bytes 811016 | tf_op jit(solution)/shard_map/ppermute | solution.py:22
  106.2 45.6 %collective-permute-start.27 = (bf16[256,512]{1,0:T(8,128)(2,1)S(1)}, bf16[256,512]{1,0:T(8,128)(2,1)}, u32[]{:S(2)}, u32[]{:S(2)}) collective-permute-start(bf16[256,512]{1,0:T(8,128)(2,1)S(1)} %pad_maximum_fusion.10.refs_1_.refs_0_), channel_id=1, source_target_pairs={{4,0},{8,4},{12,8},{0,12},{5,1},{9,5},{13,9},{1,13},{6,2},{10,6},{... | collective-permute-start | bytes 786440 | tf_op jit(solution)/shard_map/ppermute | solution.py:22
  114.5 37.9 %collective-permute-start.28 = (bf16[256,512]{1,0:T(8,128)(2,1)S(1)}, bf16[256,512]{1,0:T(8,128)(2,1)}, u32[]{:S(2)}, u32[]{:S(2)}) collective-permute-start(bf16[256,512]{1,0:T(8,128)(2,1)S(1)} %pad_maximum_fusion.10.refs_1_.refs_0_), channel_id=1, source_target_pairs={{8,0},{12,4},{0,8},{4,12},{9,1},{13,5},{1,9},{5,13},{10,2},{14,6},... | collective-permute-start | bytes 786440 | tf_op jit(solution)/shard_map/ppermute | solution.py:22
  182.8 89.5 %collective-permute-start.51 = (bf16[256,4224]{1,0:T(8,128)(2,1)S(1)}, bf16[256,4224]{1,0:T(8,128)(2,1)S(1)}, u32[]{:S(2)}, u32[]{:S(2)}) collective-permute-start(bf16[256,4224]{1,0:T(8,128)(2,1)S(1)} %pad_maximum_fusion.1.refs_4_), channel_id=1, source_target_pairs={{16,0},{32,16},{48,32},{0,48},{17,1},{33,17},{49,33},{1,49},{18,2}... | collective-permute-start | bytes 6488072 | tf_op jit(solution)/shard_map/ppermute | solution.py:22
  197.8 72.1 %collective-permute-start.39 = (bf16[128,2048]{1,0:T(8,128)(2,1)S(1)}, bf16[128,2048]{1,0:T(8,128)(2,1)S(1)}, u32[]{:S(2)}, u32[]{:S(2)}) collective-permute-start(bf16[128,2048]{1,0:T(8,128)(2,1)S(1)} %copy-done.61), channel_id=1, source_target_pairs={{2,0},{0,2},{3,1},{1,3},{6,4},{4,6},{7,5},{5,7},{10,8},{8,10},{11,... | collective-permute-start | bytes 1572872 | tf_op jit(solution)/shard_map/ppermute | solution.py:22
  198.4 65.9 %collective-permute-start.42 = (bf16[64,4224]{1,0:T(8,128)(2,1)S(1)}, bf16[64,4224]{1,0:T(8,128)(2,1)S(1)}, u32[]{:S(2)}, u32[]{:S(2)}) collective-permute-start(bf16[64,4224]{1,0:T(8,128)(2,1)S(1)} %bitcast.254), channel_id=1, source_target_pairs={{16,0},{32,16},{48,32},{0,48},{17,1},{33,17},{49,33},{1,49},{18,2}... | collective-permute-start | bytes 1622024 | tf_op jit(solution)/shard_map/ppermute | solution.py:22
  199.7 64.6 %collective-permute-start.43 = (bf16[64,4224]{1,0:T(8,128)(2,1)S(1)}, bf16[64,4224]{1,0:T(8,128)(2,1)S(1)}, u32[]{:S(2)}, u32[]{:S(2)}) collective-permute-start(bf16[64,4224]{1,0:T(8,128)(2,1)S(1)} %bitcast.255), channel_id=1, source_target_pairs={{32,0},{48,16},{0,32},{16,48},{33,1},{49,17},{1,33},{17,49},{34,2}... | collective-permute-start | bytes 1622024 | tf_op jit(solution)/shard_map/ppermute | solution.py:22
  209.8 58.6 %collective-permute-start.44 = (bf16[64,4224]{1,0:T(8,128)(2,1)S(1)}, bf16[64,4224]{1,0:T(8,128)(2,1)S(1)}, u32[]{:S(2)}, u32[]{:S(2)}) collective-permute-start(bf16[64,4224]{1,0:T(8,128)(2,1)S(1)} %bitcast.256), channel_id=1, source_target_pairs={{48,0},{0,16},{16,32},{32,48},{49,1},{1,17},{17,33},{33,49},{50,2}... | collective-permute-start | bytes 1622024 | tf_op jit(solution)/shard_map/ppermute | solution.py:22
  264.3 49.3 %collective-permute-start.52 = (bf16[256,4224]{1,0:T(8,128)(2,1)S(1)}, bf16[256,4224]{1,0:T(8,128)(2,1)S(1)}, u32[]{:S(2)}, u32[]{:S(2)}) collective-permute-start(bf16[256,4224]{1,0:T(8,128)(2,1)S(1)} %pad_maximum_fusion.1.refs_4_), channel_id=1, source_target_pairs={{32,0},{48,16},{0,32},{16,48},{33,1},{49,17},{1,33},{17,49},{34,2}... | collective-permute-start | bytes 6488072 | tf_op jit(solution)/shard_map/ppermute | solution.py:22
  264.3 96.8 %collective-permute-start.53 = (bf16[256,4224]{1,0:T(8,128)(2,1)S(1)}, bf16[256,4224]{1,0:T(8,128)(2,1)S(1)}, u32[]{:S(2)}, u32[]{:S(2)}) collective-permute-start(bf16[256,4224]{1,0:T(8,128)(2,1)S(1)} %pad_maximum_fusion.1.refs_4_), channel_id=1, source_target_pairs={{48,0},{0,16},{16,32},{32,48},{49,1},{1,17},{17,33},{33,49},{50,2}... | collective-permute-start | bytes 6488072 | tf_op jit(solution)/shard_map/ppermute | solution.py:22
  269.9 91.3 %collective-permute-start.45 = (bf16[256,4224]{1,0:T(8,128)(2,1)S(1)}, bf16[256,4224]{1,0:T(8,128)(2,1)S(1)}, u32[]{:S(2)}, u32[]{:S(2)}) collective-permute-start(bf16[256,4224]{1,0:T(8,128)(2,1)S(1)} %pad_maximum_fusion.refs_0_), channel_id=1, source_target_pairs={{4,0},{8,4},{12,8},{0,12},{5,1},{9,5},{13,9},{1,13},{6,2},{10,6},{... | collective-permute-start | bytes 6488072 | tf_op jit(solution)/shard_map/ppermute | solution.py:22
  272.4 88.8 %collective-permute-start.46 = (bf16[256,4224]{1,0:T(8,128)(2,1)S(1)}, bf16[256,4224]{1,0:T(8,128)(2,1)S(1)}, u32[]{:S(2)}, u32[]{:S(2)}) collective-permute-start(bf16[256,4224]{1,0:T(8,128)(2,1)S(1)} %pad_maximum_fusion.refs_0_), channel_id=1, source_target_pairs={{8,0},{12,4},{0,8},{4,12},{9,1},{13,5},{1,9},{5,13},{10,2},{14,6},... | collective-permute-start | bytes 6488072 | tf_op jit(solution)/shard_map/ppermute | solution.py:22
  273.9 95.3 %collective-permute-start.47 = (bf16[256,4224]{1,0:T(8,128)(2,1)S(1)}, bf16[256,4224]{1,0:T(8,128)(2,1)S(1)}, u32[]{:S(2)}, u32[]{:S(2)}) collective-permute-start(bf16[256,4224]{1,0:T(8,128)(2,1)S(1)} %pad_maximum_fusion.refs_0_), channel_id=1, source_target_pairs={{12,0},{0,4},{4,8},{8,12},{13,1},{1,5},{5,9},{9,13},{14,2},{2,6},{... | collective-permute-start | bytes 6488072 | tf_op jit(solution)/shard_map/ppermute | solution.py:22
  446.1 151.6 %collective-permute-start.97 = (bf16[256,4224]{1,0:T(8,128)(2,1)}, bf16[256,4224]{1,0:T(8,128)(2,1)}, u32[]{:S(2)}, u32[]{:S(2)}) collective-permute-start(bf16[256,4224]{1,0:T(8,128)(2,1)} %get-tuple-element.74), channel_id=1, source_target_pairs={{12,0},{0,4},{4,8},{8,12},{13,1},{1,5},{5,9},{9,13},{14,2},{2,6},{... | collective-permute-start | bytes 6488072 | tf_op jit(solution)/shard_map/ppermute | solution.py:22
  456.5 45.9 %collective-permute-start.83 = (bf16[256,512]{1,0:T(8,128)(2,1)}, bf16[256,512]{1,0:T(8,128)(2,1)}, u32[]{:S(2)}, u32[]{:S(2)}) collective-permute-start(bf16[256,512]{1,0:T(8,128)(2,1)} %get-tuple-element.66), channel_id=1, source_target_pairs={{12,0},{0,4},{4,8},{8,12},{13,1},{1,5},{5,9},{9,13},{14,2},{2,6},{... | collective-permute-start | bytes 786440 | tf_op jit(solution)/shard_map/ppermute | solution.py:22
  457.7 49.6 %collective-permute-start.84 = (bf16[256,512]{1,0:T(8,128)(2,1)}, bf16[256,512]{1,0:T(8,128)(2,1)}, u32[]{:S(2)}, u32[]{:S(2)}) collective-permute-start(bf16[256,512]{1,0:T(8,128)(2,1)} %get-tuple-element.67), channel_id=1, source_target_pairs={{8,0},{12,4},{0,8},{4,12},{9,1},{13,5},{1,9},{5,13},{10,2},{14,6},... | collective-permute-start | bytes 786440 | tf_op jit(solution)/shard_map/ppermute | solution.py:22
  461.0 58.5 %collective-permute-start.85 = (bf16[256,512]{1,0:T(8,128)(2,1)}, bf16[256,512]{1,0:T(8,128)(2,1)S(1)}, u32[]{:S(2)}, u32[]{:S(2)}) collective-permute-start(bf16[256,512]{1,0:T(8,128)(2,1)} %copy-done.41), channel_id=1, source_target_pairs={{4,0},{8,4},{12,8},{0,12},{5,1},{9,5},{13,9},{1,13},{6,2},{10,6},{... | collective-permute-start | bytes 786440 | tf_op jit(solution)/shard_map/ppermute | solution.py:22
  461.5 60.0 %collective-permute-start.89 = (bf16[256,512]{1,0:T(8,128)(2,1)}, bf16[256,512]{1,0:T(8,128)(2,1)S(1)}, u32[]{:S(2)}, u32[]{:S(2)}) collective-permute-start(bf16[256,512]{1,0:T(8,128)(2,1)} %copy-done.40), channel_id=1, source_target_pairs={{48,0},{0,16},{16,32},{32,48},{49,1},{1,17},{17,33},{33,49},{50,2}... | collective-permute-start | bytes 786440 | tf_op jit(solution)/shard_map/ppermute | solution.py:22
  507.3 35.3 %collective-permute-start.91 = (bf16[256,512]{1,0:T(8,128)(2,1)S(1)}, bf16[256,512]{1,0:T(8,128)(2,1)S(1)}, u32[]{:S(2)}, u32[]{:S(2)}) collective-permute-start(bf16[256,512]{1,0:T(8,128)(2,1)S(1)} %copy-done.37), channel_id=1, source_target_pairs={{16,0},{32,16},{48,32},{0,48},{17,1},{33,17},{49,33},{1,49},{18,2}... | collective-permute-start | bytes 786440 | tf_op jit(solution)/shard_map/ppermute | solution.py:22
  519.6 85.1 %collective-permute-start.98 = (bf16[256,4224]{1,0:T(8,128)(2,1)}, bf16[256,4224]{1,0:T(8,128)(2,1)}, u32[]{:S(2)}, u32[]{:S(2)}) collective-permute-start(bf16[256,4224]{1,0:T(8,128)(2,1)} %get-tuple-element.75), channel_id=1, source_target_pairs={{8,0},{12,4},{0,8},{4,12},{9,1},{13,5},{1,9},{5,13},{10,2},{14,6},... | collective-permute-start | bytes 6488072 | tf_op jit(solution)/shard_map/ppermute | solution.py:22
  572.4 48.4 %collective-permute-start.99 = (bf16[256,4224]{1,0:T(8,128)(2,1)}, bf16[256,4224]{1,0:T(8,128)(2,1)}, u32[]{:S(2)}, u32[]{:S(2)}) collective-permute-start(bf16[256,4224]{1,0:T(8,128)(2,1)} %get-tuple-element.76), channel_id=1, source_target_pairs={{4,0},{8,4},{12,8},{0,12},{5,1},{9,5},{13,9},{1,13},{6,2},{10,6},{... | collective-permute-start | bytes 6488072 | tf_op jit(solution)/shard_map/ppermute | solution.py:22
  572.4 66.2 %collective-permute-start.103 = (bf16[256,4224]{1,0:T(8,128)(2,1)}, bf16[256,4224]{1,0:T(8,128)(2,1)}, u32[]{:S(2)}, u32[]{:S(2)}) collective-permute-start(bf16[256,4224]{1,0:T(8,128)(2,1)} %get-tuple-element.78), channel_id=1, source_target_pairs={{48,0},{0,16},{16,32},{32,48},{49,1},{1,17},{17,33},{33,49},{50,2}... | collective-permute-start | bytes 6488072 | tf_op jit(solution)/shard_map/ppermute | solution.py:22
  584.5 101.4 %collective-permute-start.104 = (bf16[256,4224]{1,0:T(8,128)(2,1)}, bf16[256,4224]{1,0:T(8,128)(2,1)}, u32[]{:S(2)}, u32[]{:S(2)}) collective-permute-start(bf16[256,4224]{1,0:T(8,128)(2,1)} %get-tuple-element.79), channel_id=1, source_target_pairs={{32,0},{48,16},{0,32},{16,48},{33,1},{49,17},{1,33},{17,49},{34,2}... | collective-permute-start | bytes 6488072 | tf_op jit(solution)/shard_map/ppermute | solution.py:22
  597.6 94.6 %collective-permute-start.105 = (bf16[256,4224]{1,0:T(8,128)(2,1)}, bf16[256,4224]{1,0:T(8,128)(2,1)}, u32[]{:S(2)}, u32[]{:S(2)}) collective-permute-start(bf16[256,4224]{1,0:T(8,128)(2,1)} %get-tuple-element.80), channel_id=1, source_target_pairs={{16,0},{32,16},{48,32},{0,48},{17,1},{33,17},{49,33},{1,49},{18,2}... | collective-permute-start | bytes 6488072 | tf_op jit(solution)/shard_map/ppermute | solution.py:22
  604.7 95.5 %collective-permute-start.59 = (bf16[4096,128]{1,0:T(8,128)(2,1)}, bf16[4096,128]{1,0:T(8,128)(2,1)S(1)}, u32[]{:S(2)}, u32[]{:S(2)}) collective-permute-start(bf16[4096,128]{1,0:T(8,128)(2,1)} %select_convert_fusion), channel_id=1, source_target_pairs={{2,0},{0,2},{3,1},{1,3},{6,4},{4,6},{7,5},{5,7},{10,8},{8,10},{11,... | collective-permute-start | bytes 3145736 | tf_op jit(solution)/shard_map/ppermute | solution.py:22
  620.9 134.5 %collective-permute-start.96 = (f32[32,512]{1,0:T(8,128)S(1)}, f32[32,512]{1,0:T(8,128)S(1)}, u32[]{:S(2)}, u32[]{:S(2)}) collective-permute-start(f32[32,512]{1,0:T(8,128)S(1)} %get-tuple-element.167), channel_id=1, source_target_pairs={{2,0},{0,2},{3,1},{1,3},{6,4},{4,6},{7,5},{5,7},{10,8},{8,10},{11,... | collective-permute-start | bytes 196616 | tf_op jit(solution)/shard_map/ppermute | solution.py:22
  638.6 63.0 %collective-permute-start.100 = (bf16[64,4224]{1,0:T(8,128)(2,1)S(1)}, bf16[64,4224]{1,0:T(8,128)(2,1)S(1)}, u32[]{:S(2)}, u32[]{:S(2)}) collective-permute-start(bf16[64,4224]{1,0:T(8,128)(2,1)S(1)} %get-tuple-element.100), channel_id=1, source_target_pairs={{48,0},{0,16},{16,32},{32,48},{49,1},{1,17},{17,33},{33,49},{50,2}... | collective-permute-start | bytes 1622024 | tf_op jit(solution)/shard_map/ppermute | solution.py:22
  (184 other events, 3024.7 us)
